TPU v7x, 32 devices: a whole 2x2x4 slice. The times are simulated.
32 devices in a mesh: fsdp: 8 (over z, core), expert: 4 (over y, x).
Axes of the slice: x: 2, y: 2, z: 4, core: 2. Of those that a mesh axis runs over, the one named last changes fastest.
Arguments:
- tokens: bfloat16 [2, 2048, 1024], P(None, ('fsdp', 'expert')), may hold values from -6 to 6
- segments: int32 [2, 32, 64], P(None, ('fsdp', 'expert')), may hold values from 0 to 3, never falling along the last dimension, each value on 1 to 32 neighbouring positions
- routes: int32 [2, 2048, 8], P(None, ('fsdp', 'expert')), may hold values from 0 to 15, all different within a row; in each aligned block of 64 rows (0 to 63, 64 to 127, ..., all dimensions but the last counted through in order) at most 36 rows name the same one
- cotangent: bfloat16 [2, 2048, 1024], P(None, ('fsdp', 'expert')), may hold values from -6 to 6
- gain_attn: bfloat16 [1024], P(('fsdp', 'expert')), may hold values from 0.5 to 1.5
- w_query: bfloat16 [1024, 1024], P(('fsdp', 'expert')), may hold values from -0.1875 to 0.1875
- w_key: bfloat16 [1024, 512], P(('fsdp', 'expert')), may hold values from -0.1875 to 0.1875
- w_value: bfloat16 [1024, 512], P(('fsdp', 'expert')), may hold values from -0.1875 to 0.1875
- w_out: bfloat16 [1024, 1024], P(('fsdp', 'expert')), may hold values from -0.5 to 0.5
- gain_moe: bfloat16 [1024], P(('fsdp', 'expert')), may hold values from 0.5 to 1.5
- w_router: bfloat16 [1024, 16], P(('fsdp', 'expert')), may hold values from -0.09375 to 0.09375
- expert_gate: bfloat16 [16, 1024, 512], P('expert', 'fsdp'), may hold values from -0.1875 to 0.1875
- expert_up: bfloat16 [16, 1024, 512], P('expert', 'fsdp'), may hold values from -0.1875 to 0.1875
- expert_down: bfloat16 [16, 1024, 512], P('expert', 'fsdp'), may hold values from -0.75 to 0.75
Outputs:
- result: bfloat16 [2, 2048, 1024], P(None, ('fsdp', 'expert'))
- grad_tokens: float32 [2, 2048, 1024], P(None, ('fsdp', 'expert'))
- grad_gain_attn: float32 [1024], P(('fsdp', 'expert'))
- grad_w_query: float32 [1024, 1024], P(('fsdp', 'expert'))
- grad_w_key: float32 [1024, 512], P(('fsdp', 'expert'))
- grad_w_value: float32 [1024, 512], P(('fsdp', 'expert'))
- grad_w_out: float32 [1024, 1024], P(('fsdp', 'expert'))
- grad_gain_moe: float32 [1024], P(('fsdp', 'expert'))
- grad_w_router: float32 [1024, 16], P(('fsdp', 'expert'))
- grad_expert_gate: float32 [16, 1024, 512], P('expert', 'fsdp')
- grad_expert_up: float32 [16, 1024, 512], P('expert', 'fsdp')
- grad_expert_down: float32 [16, 1024, 512], P('expert', 'fsdp')
Inputs may be any that keep to these rules, and one draw needn't show every extreme that they name: `routes`: each row names 8 different experts; within the tokens of one sequence no expert is named more than 36 times. `segments`: within a sequence the numbers never fall; each document holds 1 to 32 tokens.
All inputs are finite; a program needn't handle non-finite values.
Results may differ from a plain program's by a relative error of at most 0.015.
Values may be sent and summed in bfloat16 or wider, within the bound.
A program may use at most 128 MiB of HBM per device.

v0:
```python
import jax
import jax.numpy as jnp
from jax import lax
from jax.sharding import PartitionSpec as P

HEADS = 16
KV_HEADS = 8
HEAD_DIM = 64
EXPERTS = 16
TOP = 8
CAP = 36


EPS = 1e-06


def root_mean(values, gain):
    inverse = lax.rsqrt(jnp.mean(values * values, -1, keepdims=True) + EPS)
    return (values * inverse * gain, inverse)


def norm_back(grad, values, inverse, gain):
    unit = values * inverse
    scaled = grad * gain
    back = inverse * (scaled - unit * jnp.mean(scaled * unit, -1, keepdims=True))
    return (back, jnp.sum(grad * unit, 0))


def rotate(values, direction):
    half = HEAD_DIM // 2
    places = jnp.arange(values.shape[0], dtype=jnp.float32)
    rates = 10000.0 ** (-jnp.arange(half, dtype=jnp.float32) * 2.0 / HEAD_DIM)
    angle = places[:, None] * rates[None, :]
    cosine = jnp.cos(angle)[:, None, :]
    sine = direction * jnp.sin(angle)[:, None, :]
    first = values[..., :half]
    second = values[..., half:]
    return jnp.concatenate([first * cosine - second * sine, second * cosine + first * sine], -1)


def slot_table(route):
    flat = route.reshape(-1)
    hits = (flat[:, None] == jnp.arange(EXPERTS, dtype=jnp.int32)[None, :]).astype(jnp.int32)
    before = jnp.cumsum(hits, axis=0) - hits
    position = jnp.sum(before * hits, axis=1)
    slot = flat * CAP + position
    table = (slot[:, None] == jnp.arange(EXPERTS * CAP, dtype=jnp.int32)[None, :]).astype(
        jnp.float32
    )
    return (slot, table.reshape(route.shape[0], route.shape[1], EXPERTS * CAP))


def inner(left, right):
    return lax.dot_general(
        left, right, (((0,), (0,)), ((), ())), preferred_element_type=jnp.float32
    )


def outer_back(left, right):
    return lax.dot_general(
        left, right, (((1,), (1,)), ((), ())), preferred_element_type=jnp.float32
    )


def attention_scores(query, key, allowed):
    raw = jnp.einsum(
        "sgrd,tgd->grst", query, key, preferred_element_type=jnp.float32
    ) * HEAD_DIM ** (-0.5)
    return jnp.where(allowed[None, None], raw, -1e30)


def per_device(
    tokens,
    segments,
    routes,
    cotangent,
    gain_attn,
    w_query,
    w_key,
    w_value,
    w_out,
    gain_moe,
    w_router,
    expert_gate,
    expert_up,
    expert_down,
):
    micro, length, width = tokens.shape
    repeat = HEADS // KV_HEADS
    scale = HEAD_DIM ** (-0.5)
    highest = lax.Precision.HIGHEST
    dense_kept = (
        lax.all_gather(gain_attn, ("fsdp", "expert"), axis=0, tiled=True),
        lax.all_gather(w_query, ("fsdp", "expert"), axis=0, tiled=True),
        lax.all_gather(w_key, ("fsdp", "expert"), axis=0, tiled=True),
        lax.all_gather(w_value, ("fsdp", "expert"), axis=0, tiled=True),
        lax.all_gather(w_out, ("fsdp", "expert"), axis=0, tiled=True),
        lax.all_gather(gain_moe, ("fsdp", "expert"), axis=0, tiled=True),
        lax.all_gather(w_router, ("fsdp", "expert"), axis=0, tiled=True),
    )
    expert_kept = (
        lax.all_gather(expert_gate, "fsdp", axis=1, tiled=True),
        lax.all_gather(expert_up, "fsdp", axis=1, tiled=True),
        lax.all_gather(expert_down, "fsdp", axis=1, tiled=True),
    )
    outputs_all = []
    grads_all = []
    kept_first_in = []
    kept_query_grad = []
    kept_key_grad = []
    kept_value_grad = []
    kept_context = []
    kept_branch = []
    kept_second_in = []
    kept_logit_grad = []
    kept_arrived = []
    kept_gate_back = []
    kept_up_back = []
    kept_slot_grad = []
    kept_hidden = []
    first_gain_total = None
    second_gain_total = None
    places = jnp.arange(length, dtype=jnp.int32)
    expert_ids = jnp.arange(EXPERTS, dtype=jnp.int32)
    for index in range(micro):
        (
            first_gain,
            query_weight,
            key_weight,
            value_weight,
            out_weight,
            second_gain,
            router_weight,
        ) = dense_kept
        first_gain = first_gain.astype(jnp.float32)
        second_gain = second_gain.astype(jnp.float32)
        source = tokens[index].astype(jnp.float32)
        segment = segments[index, 0]
        route = routes[index]
        allowed = (places[:, None] >= places[None, :]) & (segment[:, None] == segment[None, :])
        first_norm, first_inverse = root_mean(source, first_gain)
        first_in = first_norm.astype(jnp.bfloat16)
        query_pre = jnp.dot(first_in, query_weight, preferred_element_type=jnp.float32).reshape(
            length, HEADS, HEAD_DIM
        )
        key_pre = jnp.dot(first_in, key_weight, preferred_element_type=jnp.float32).reshape(
            length, KV_HEADS, HEAD_DIM
        )
        value = (
            jnp.dot(first_in, value_weight, preferred_element_type=jnp.float32)
            .astype(jnp.bfloat16)
            .reshape(length, KV_HEADS, HEAD_DIM)
        )
        query = (
            rotate(query_pre, 1.0).astype(jnp.bfloat16).reshape(length, KV_HEADS, repeat, HEAD_DIM)
        )
        key = rotate(key_pre, 1.0).astype(jnp.bfloat16)
        scores = attention_scores(query, key, allowed)
        peak = jnp.max(scores, -1, keepdims=True)
        total = jnp.log(jnp.sum(jnp.exp(scores - peak), -1, keepdims=True)) + peak
        probs = jnp.exp(scores - total)
        context = jnp.einsum(
            "grst,tgd->sgrd", probs.astype(jnp.bfloat16), value, preferred_element_type=jnp.float32
        )
        context = context.reshape(length, HEADS * HEAD_DIM).astype(jnp.bfloat16)
        mixed = source + jnp.dot(context, out_weight, preferred_element_type=jnp.float32)
        second_norm, second_inverse = root_mean(mixed, second_gain)
        second_in = second_norm.astype(jnp.bfloat16)
        router_full = router_weight.astype(jnp.float32)
        logits = jnp.dot(second_in.astype(jnp.float32), router_full, precision=highest)
        chosen = jnp.take_along_axis(logits, route, axis=1)
        gates = jax.nn.softmax(chosen, axis=-1)
        slot, table = slot_table(route)
        place = jnp.sum(table, 1).astype(jnp.bfloat16)
        send = inner(place, second_in).astype(jnp.bfloat16).reshape(EXPERTS, CAP, width)
        arrived = lax.all_to_all(send, "expert", split_axis=0, concat_axis=1, tiled=True)
        gate_full, up_full, down_full = expert_kept
        gate = jnp.einsum("erd,edf->erf", arrived, gate_full, preferred_element_type=jnp.float32)
        up = jnp.einsum("erd,edf->erf", arrived, up_full, preferred_element_type=jnp.float32)
        hidden = (jax.nn.silu(gate) * up).astype(jnp.bfloat16)
        produced = jnp.einsum(
            "erf,edf->erd", hidden, down_full, preferred_element_type=jnp.float32
        ).astype(jnp.bfloat16)
        returned = lax.all_to_all(
            produced, "expert", split_axis=1, concat_axis=0, tiled=True
        ).reshape(EXPERTS * CAP, width)
        picked = jnp.take(returned, slot, axis=0).reshape(length, TOP, width).astype(jnp.float32)
        result = mixed + jnp.sum(gates[:, :, None] * picked, 1)
        outputs_all.append(result.astype(jnp.bfloat16))
        upstream = cotangent[index].astype(jnp.float32)
        (
            first_gain,
            query_weight,
            key_weight,
            value_weight,
            out_weight,
            second_gain,
            router_weight,
        ) = dense_kept
        first_gain = first_gain.astype(jnp.float32)
        second_gain = second_gain.astype(jnp.float32)
        router_full = router_weight.astype(jnp.float32)
        weighted = (
            (gates[:, :, None] * upstream[:, None, :])
            .astype(jnp.bfloat16)
            .reshape(length * TOP, width)
        )
        flat_table = table.reshape(length * TOP, EXPERTS * CAP).astype(jnp.bfloat16)
        slot_grad = inner(flat_table, weighted).astype(jnp.bfloat16).reshape(EXPERTS, CAP, width)
        gate_grad = jnp.einsum("skd,sd->sk", picked, upstream, precision=highest)
        chosen_grad = gates * (gate_grad - jnp.sum(gates * gate_grad, -1, keepdims=True))
        expert_hits = (route[:, :, None] == expert_ids[None, None, :]).astype(jnp.float32)
        logit_grad = jnp.sum(chosen_grad[:, :, None] * expert_hits, 1)
        router_in_grad = jnp.dot(logit_grad, router_full.T, precision=highest)
        slot_grad_in = lax.all_to_all(slot_grad, "expert", split_axis=0, concat_axis=1, tiled=True)
        gate_full, up_full, down_full = expert_kept
        hidden_grad = jnp.einsum(
            "erd,edf->erf", slot_grad_in, down_full, preferred_element_type=jnp.float32
        )
        sigma = jax.nn.sigmoid(gate)
        gate_back = (hidden_grad * up * sigma * (1.0 + gate * (1.0 - sigma))).astype(jnp.bfloat16)
        up_back = (hidden_grad * gate * sigma).astype(jnp.bfloat16)
        input_back = jnp.einsum(
            "erf,edf->erd", gate_back, gate_full, preferred_element_type=jnp.float32
        )
        input_back = (
            input_back
            + jnp.einsum("erf,edf->erd", up_back, up_full, preferred_element_type=jnp.float32)
        ).astype(jnp.bfloat16)
        input_home = lax.all_to_all(
            input_back, "expert", split_axis=1, concat_axis=0, tiled=True
        ).reshape(EXPERTS * CAP, width)
        second_grad = (
            jnp.dot(place, input_home, preferred_element_type=jnp.float32) + router_in_grad
        )
        mixed_back, second_gain_grad = norm_back(second_grad, mixed, second_inverse, second_gain)
        mixed_grad = upstream + mixed_back
        branch_grad = mixed_grad.astype(jnp.bfloat16)
        context_grad = (
            outer_back(branch_grad, out_weight)
            .astype(jnp.bfloat16)
            .reshape(length, KV_HEADS, repeat, HEAD_DIM)
        )
        scores = attention_scores(query, key, allowed)
        probs = jnp.exp(scores - total)
        value_grad = jnp.einsum(
            "grst,sgrd->tgd",
            probs.astype(jnp.bfloat16),
            context_grad,
            preferred_element_type=jnp.float32,
        )
        value_grad = value_grad.astype(jnp.bfloat16).reshape(length, KV_HEADS * HEAD_DIM)
        prob_grad = jnp.einsum(
            "sgrd,tgd->grst", context_grad, value, preferred_element_type=jnp.float32
        )
        score_grad = (probs * (prob_grad - jnp.sum(probs * prob_grad, -1, keepdims=True))).astype(
            jnp.bfloat16
        )
        query_grad = (
            jnp.einsum("grst,tgd->sgrd", score_grad, key, preferred_element_type=jnp.float32)
            * scale
        )
        key_grad = (
            jnp.einsum("grst,sgrd->tgd", score_grad, query, preferred_element_type=jnp.float32)
            * scale
        )
        query_pre_grad = (
            rotate(query_grad.reshape(length, HEADS, HEAD_DIM), -1.0)
            .astype(jnp.bfloat16)
            .reshape(length, HEADS * HEAD_DIM)
        )
        key_pre_grad = (
            rotate(key_grad, -1.0).astype(jnp.bfloat16).reshape(length, KV_HEADS * HEAD_DIM)
        )
        first_grad = (
            outer_back(query_pre_grad, query_weight)
            + outer_back(key_pre_grad, key_weight)
            + outer_back(value_grad, value_weight)
        )
        source_back, first_gain_grad = norm_back(first_grad, source, first_inverse, first_gain)
        grads_all.append(mixed_grad + source_back)
        kept_first_in.append(first_in)
        kept_query_grad.append(query_pre_grad)
        kept_key_grad.append(key_pre_grad)
        kept_value_grad.append(value_grad)
        kept_context.append(context)
        kept_branch.append(branch_grad)
        kept_second_in.append(second_in.astype(jnp.float32))
        kept_logit_grad.append(logit_grad)
        kept_arrived.append(arrived)
        kept_gate_back.append(gate_back)
        kept_up_back.append(up_back)
        kept_slot_grad.append(slot_grad_in)
        kept_hidden.append(hidden)
        if first_gain_total is None:
            first_gain_total = first_gain_grad
            second_gain_total = second_gain_grad
        else:
            first_gain_total = first_gain_total + first_gain_grad
            second_gain_total = second_gain_total + second_gain_grad
    first_rows = jnp.concatenate(kept_first_in, 0)
    dense_total = (
        first_gain_total,
        inner(first_rows, jnp.concatenate(kept_query_grad, 0)),
        inner(first_rows, jnp.concatenate(kept_key_grad, 0)),
        inner(first_rows, jnp.concatenate(kept_value_grad, 0)),
        inner(jnp.concatenate(kept_context, 0), jnp.concatenate(kept_branch, 0)),
        second_gain_total,
        jnp.dot(
            jnp.concatenate(kept_second_in, 0).T,
            jnp.concatenate(kept_logit_grad, 0),
            precision=highest,
        ),
    )
    arrived_rows = jnp.concatenate(kept_arrived, 1)
    expert_total = (
        jnp.einsum(
            "erd,erf->edf",
            arrived_rows,
            jnp.concatenate(kept_gate_back, 1),
            preferred_element_type=jnp.float32,
        ),
        jnp.einsum(
            "erd,erf->edf",
            arrived_rows,
            jnp.concatenate(kept_up_back, 1),
            preferred_element_type=jnp.float32,
        ),
        jnp.einsum(
            "erd,erf->edf",
            jnp.concatenate(kept_slot_grad, 1),
            jnp.concatenate(kept_hidden, 1),
            preferred_element_type=jnp.float32,
        ),
    )
    dense_parts = (
        lax.psum_scatter(dense_total[0], ("fsdp", "expert"), scatter_dimension=0, tiled=True),
        lax.psum_scatter(dense_total[1], ("fsdp", "expert"), scatter_dimension=0, tiled=True),
        lax.psum_scatter(dense_total[2], ("fsdp", "expert"), scatter_dimension=0, tiled=True),
        lax.psum_scatter(dense_total[3], ("fsdp", "expert"), scatter_dimension=0, tiled=True),
        lax.psum_scatter(dense_total[4], ("fsdp", "expert"), scatter_dimension=0, tiled=True),
        lax.psum_scatter(dense_total[5], ("fsdp", "expert"), scatter_dimension=0, tiled=True),
        lax.psum_scatter(dense_total[6], ("fsdp", "expert"), scatter_dimension=0, tiled=True),
    )
    expert_parts = (
        lax.psum_scatter(
            expert_total[0].astype(jnp.bfloat16), "fsdp", scatter_dimension=1, tiled=True
        ).astype(jnp.float32),
        lax.psum_scatter(
            expert_total[1].astype(jnp.bfloat16), "fsdp", scatter_dimension=1, tiled=True
        ).astype(jnp.float32),
        lax.psum_scatter(
            expert_total[2].astype(jnp.bfloat16), "fsdp", scatter_dimension=1, tiled=True
        ).astype(jnp.float32),
    )
    return (
        jnp.stack(outputs_all),
        jnp.stack(grads_all),
        dense_parts[0],
        dense_parts[1],
        dense_parts[2],
        dense_parts[3],
        dense_parts[4],
        dense_parts[5],
        dense_parts[6],
        expert_parts[0],
        expert_parts[1],
        expert_parts[2],
    )


def solution(mesh):
    placed = (
        P(None, ("fsdp", "expert"), None),
        P(None, ("fsdp", "expert"), None),
        P(None, ("fsdp", "expert"), None),
        P(None, ("fsdp", "expert"), None),
        P(("fsdp", "expert")),
        P(("fsdp", "expert"), None),
        P(("fsdp", "expert"), None),
        P(("fsdp", "expert"), None),
        P(("fsdp", "expert"), None),
        P(("fsdp", "expert")),
        P(("fsdp", "expert"), None),
        P("expert", "fsdp", None),
        P("expert", "fsdp", None),
        P("expert", "fsdp", None),
    )
    return jax.shard_map(
        per_device,
        mesh=mesh,
        in_specs=placed,
        out_specs=(
            P(None, ("fsdp", "expert"), None),
            P(None, ("fsdp", "expert"), None),
            P(("fsdp", "expert")),
            P(("fsdp", "expert"), None),
            P(("fsdp", "expert"), None),
            P(("fsdp", "expert"), None),
            P(("fsdp", "expert"), None),
            P(("fsdp", "expert")),
            P(("fsdp", "expert"), None),
            P("expert", "fsdp", None),
            P("expert", "fsdp", None),
            P("expert", "fsdp", None),
        ),
        check_vma=False,
    )
```

profile of v0, /device:TPU:0, one launch (start us, length us, event | category | flops | bytes accessed | tf_op | source)
XLA Modules:
  0.0 1397.3 jit_solution(11108447837319695420)
XLA Ops:
  17.3 42.0 %all-reduce.5 = (bf16[1024]{0:T(1024)(128)(2,1)S(1)}, bf16[1024]{0:T(1024)(128)(2,1)S(1)}) all-reduce(bf16[1024]{0:T(1024)(128)(2,1)S(1)} %dynamic-update-slice, bf16[1024]{0:T(1024)(128)(2,1)S(1)} %dynamic-update-slice.1), channel_id=1, replica_groups=mesh['fsdp'=8,'expert'=4] {'fsdp','expert'}, use_global_device_ids=true, to_apply=%add | all-reduce | flops 2048 | bytes 8192
  62.1 5.8 all-gather.9.cloned.1.call-done
  69.5 53.9 %all-gather.11.cloned.1.call-done = bf16[1024,512]{1,0:T(8,128)(2,1)} async-done(((bf16[32,512]{1,0:T(8,128)(2,1)}), bf16[1024,512]{1,0:T(8,128)(2,1)}) %all-gather.11.cloned.1.call-update) | async-done | bytes 1048592 | tf_op jit(solution)/shard_map/all_gather | solution.py:95
  126.0 55.7 %all-gather.13.cloned.1.call-done = bf16[1024,1024]{1,0:T(8,128)(2,1)} async-done(((bf16[32,1024]{1,0:T(8,128)(2,1)}), bf16[1024,1024]{1,0:T(8,128)(2,1)}) %all-gather.13.cloned.1.call-update) | async-done | bytes 2097168 | tf_op jit(solution)/shard_map/all_gather | solution.py:94
  188.2 51.4 %all-gather.15.cloned.1.call-done = bf16[1024,1024]{1,0:T(8,128)(2,1)} async-done(((bf16[32,1024]{1,0:T(8,128)(2,1)}), bf16[1024,1024]{1,0:T(8,128)(2,1)}) %all-gather.15.cloned.1.call-update) | async-done | bytes 2097168 | tf_op jit(solution)/shard_map/all_gather | solution.py:97
  247.7 77.6 %all-gather = bf16[32,32,16]{1,2,0:T(8,128)(2,1)S(1)} all-gather(bf16[1,32,16]{1,2,0:T(8,128)(2,1)S(1)} %bitcast.487), channel_id=1, replica_groups=mesh['fsdp'=8,'expert'=4] {'fsdp','expert'}, dimensions={0}, use_global_device_ids=true | all-gather | bytes 33792 | tf_op jit(solution)/shard_map/all_gather | solution.py:99
  330.0 4.7 fusion.42
  335.0 4.9 multiply_convert_fusion.5
  339.9 42.8 %all-gather.21.cloned.1.call-done = bf16[4,1024,512]{2,1,0:T(8,128)(2,1)} async-done(((bf16[4,128,512]{2,1,0:T(8,128)(2,1)}), bf16[4,1024,512]{2,1,0:T(8,128)(2,1)}) %all-gather.21.cloned.1.call-update) | async-done | bytes 4194320 | tf_op jit(solution)/shard_map/all_gather | solution.py:104
  393.3 3.9 gather_fusion
  397.6 10.3 all-to-all-done.1
  418.7 4.6 all-to-all-start.4
  426.1 13.4 all-to-all-done.4
  441.8 4.1 multiply_convert_fusion.2
  452.1 4.4 all-to-all-start.5
  457.8 13.3 all-to-all-done.5
  481.8 20.4 %all_to_all.132 = bf16[16,36,1024]{2,1,0:T(8,128)(2,1)S(1)} all-to-all(bf16[16,36,1024]{2,1,0:T(8,128)(2,1)} %reshape.506), channel_id=1, replica_groups=mesh['fsdp'=8,'expert'=4] {'expert'}, dimensions={0} | all-to-all | bytes 2359296 | tf_op jit(solution)/shard_map/all_to_all | solution.py:176
  540.9 4.4 all-to-all-start.6
  550.4 11.6 all-to-all-done.6
  566.3 4.3 convolution_convert_fusion
  574.5 4.7 multiply_convert_fusion
  579.2 4.4 convolution_convert_fusion.1
  584.7 6.2 convolution_convert_fusion.2
  606.3 11.6 all-to-all-done.7
  647.9 35.9 %reduce-scatter.25.cloned.1.call-done = f32[32,16]{1,0:T(8,128)} async-done(((f32[1024,16]{1,0:T(8,128)}), f32[32,16]{1,0:T(8,128)}) %reduce-scatter.25.cloned.1.call-update) | async-done | bytes 2064
  689.9 38.7 %all-reduce.4 = (f32[1024]{0:T(1024)S(1)}, f32[1024]{0:T(1024)S(1)}) all-reduce(f32[1024]{0:T(1024)S(1)} %add.231, f32[1024]{0:T(1024)S(1)} %add.232), channel_id=2, replica_groups=mesh['fsdp'=8,'expert'=4] {'fsdp','expert'}, use_global_device_ids=true, to_apply=%region_34.37.clone | all-reduce | flops 2048 | bytes 16384
  735.4 48.3 %reduce-scatter.21.cloned.1.call-done = bf16[4,128,512]{2,1,0:T(8,128)(2,1)} async-done(((bf16[4,1024,512]{2,1,0:T(8,128)(2,1)}), bf16[4,128,512]{2,1,0:T(8,128)(2,1)}) %reduce-scatter.21.cloned.1.call-update) | async-done | bytes 524304 | tf_op jit(solution)/shard_map/reduce_scatter | solution.py:349
  785.8 48.5 %reduce-scatter.19.cloned.1.call-done = bf16[4,128,512]{2,1,0:T(8,128)(2,1)} async-done(((bf16[4,1024,512]{2,1,0:T(8,128)(2,1)}), bf16[4,128,512]{2,1,0:T(8,128)(2,1)}) %reduce-scatter.19.cloned.1.call-update) | async-done | bytes 524304 | tf_op jit(solution)/shard_map/reduce_scatter | solution.py:346
  836.4 136.0 %reduce-scatter.15.cloned.1.call-done = f32[32,512]{1,0:T(8,128)} async-done(((f32[1024,512]{1,0:T(8,128)}), f32[32,512]{1,0:T(8,128)}) %reduce-scatter.15.cloned.1.call-update) | async-done | bytes 65552 | tf_op jit(solution)/shard_map/reduce_scatter | solution.py:340
  972.4 135.7 %reduce-scatter.13.cloned.1.call-done = f32[32,512]{1,0:T(8,128)} async-done(((f32[1024,512]{1,0:T(8,128)}), f32[32,512]{1,0:T(8,128)}) %reduce-scatter.13.cloned.1.call-update) | async-done | bytes 65552 | tf_op jit(solution)/shard_map/reduce_scatter | solution.py:339
  1108.1 140.3 %reduce-scatter.11.cloned.1.call-done = f32[32,1024]{1,0:T(8,128)} async-done(((f32[1024,1024]{1,0:T(8,128)}), f32[32,1024]{1,0:T(8,128)}) %reduce-scatter.11.cloned.1.call-update) | async-done | bytes 131088 | tf_op jit(solution)/shard_map/reduce_scatter | solution.py:338
  1248.3 142.2 %reduce-scatter.17.cloned.1.call-done = f32[32,1024]{1,0:T(8,128)} async-done(((f32[1024,1024]{1,0:T(8,128)}), f32[32,1024]{1,0:T(8,128)}) %reduce-scatter.17.cloned.1.call-update) | async-done | bytes 131088 | tf_op jit(solution)/shard_map/reduce_scatter | solution.py:341
  (544 shorter events, 195.3 us)
Async XLA Ops:
  7.2 60.7 %all-gather.9.cloned.1.call-start = ((), (), s32[]{:S(2)}) async-start(), calls=%async_computation.16 | async-start | bytes 1081344 | tf_op jit(solution)/shard_map/all_gather | solution.py:96
  7.9 115.4 %all-gather.11.cloned.1.call-start = ((), (), s32[]{:S(2)}) async-start(), calls=%async_computation.17 | async-start | bytes 1081344 | tf_op jit(solution)/shard_map/all_gather | solution.py:95
  8.7 173.0 %all-gather.13.cloned.1.call-start = ((), (), s32[]{:S(2)}) async-start(), calls=%async_computation.18 | async-start | bytes 2162688 | tf_op jit(solution)/shard_map/all_gather | solution.py:94
  9.4 230.2 %all-gather.15.cloned.1.call-start = ((), (), s32[]{:S(2)}) async-start(), calls=%async_computation.19 | async-start | bytes 2162688 | tf_op jit(solution)/shard_map/all_gather | solution.py:97
  10.0 320.0 %all-gather.17.cloned.1.call-start = ((), (), s32[]{:S(2)}) async-start(), calls=%async_computation.20 | async-start | bytes 4718592 | tf_op jit(solution)/shard_map/all_gather | solution.py:102
  10.6 324.4 %all-gather.19.cloned.1.call-start = ((), (), s32[]{:S(2)}) async-start(), calls=%async_computation.21 | async-start | bytes 4718592 | tf_op jit(solution)/shard_map/all_gather | solution.py:103
  11.2 371.5 %all-gather.21.cloned.1.call-start = ((), (), s32[]{:S(2)}) async-start(), calls=%async_computation.22 | async-start | bytes 4718592 | tf_op jit(solution)/shard_map/all_gather | solution.py:104
  14.7 377.6 %copy-start.57 = (s32[1,64,8]{2,1,0:T(8,128)}, s32[1,64,8]{2,1,0:T(8,128)S(1)}, u32[]{:S(2)}) copy-start(s32[1,64,8]{2,1,0:T(8,128)S(1)} %copy.278) | copy-start | bytes 6148
  59.3 126.0 %copy-start.101 = (f32[1024]{0:T(1024)}, f32[1024]{0:T(1024)S(1)}, u32[]{:S(2)}) copy-start(f32[1024]{0:T(1024)S(1)} %convert_element_type.288) | copy-start | bytes 12292
  59.3 182.6 %copy-start.107 = (f32[1024]{0:T(1024)}, f32[1024]{0:T(1024)S(1)}, u32[]{:S(2)}) copy-start(f32[1024]{0:T(1024)S(1)} %convert_element_type.298) | copy-start | bytes 12292
  59.9 125.4 %copy-start.123 = (f32[64]{0:T(128)}, f32[64]{0:T(128)S(1)}, u32[]{:S(2)}) copy-start(f32[64]{0:T(128)S(1)} %get-tuple-element.107) | copy-start | bytes 772
  62.1 362.3 %copy-start.33 = (bf16[64,1024]{1,0:T(8,128)(2,1)}, bf16[64,1024]{1,0:T(8,128)(2,1)S(1)}, u32[]{:S(2)}) copy-start(bf16[64,1024]{1,0:T(8,128)(2,1)S(1)} %get-tuple-element.61) | copy-start | bytes 393220
  126.0 299.3 %copy-start.84 = (bf16[64,8,32]{0,2,1:T(8,128)(2,1)}, bf16[64,8,32]{0,2,1:T(8,128)(2,1)S(1)}, u32[]{:S(2)}) copy-start(bf16[64,8,32]{0,2,1:T(8,128)(2,1)S(1)} %get-tuple-element.75) | copy-start | bytes 98308
  126.0 299.3 %copy-start.86 = (bf16[64,8,32]{0,2,1:T(8,128)(2,1)}, bf16[64,8,32]{0,2,1:T(8,128)(2,1)S(1)}, u32[]{:S(2)}) copy-start(bf16[64,8,32]{0,2,1:T(8,128)(2,1)S(1)} %get-tuple-element.76) | copy-start | bytes 98308
  241.9 235.8 %copy-start.20 = (f32[64,1024]{1,0:T(8,128)}, f32[64,1024]{1,0:T(8,128)S(1)}, u32[]{:S(2)}) copy-start(f32[64,1024]{1,0:T(8,128)S(1)} %get-tuple-element.90) | copy-start | bytes 786436
  242.0 151.1 %copy-start.59 = (bf16[64,1024]{1,0:T(8,128)(2,1)}, bf16[64,1024]{1,0:T(8,128)(2,1)S(1)}, u32[]{:S(2)}) copy-start(bf16[64,1024]{1,0:T(8,128)(2,1)S(1)} %multiply_convert_fusion.9) | copy-start | bytes 393220
  243.7 83.0 %all-to-all-start = ((bf16[16,36,1024]{2,1,0:T(8,128)(2,1)}), bf16[16,36,1024]{2,1,0:T(8,128)(2,1)S(1)}, u32[]{:S(2)}, u32[]{:S(2)}) async-start(bf16[16,36,1024]{2,1,0:T(8,128)(2,1)} %reshape.501), calls=%async_computation | async-start | bytes 2621440 | tf_op jit(solution)/shard_map/all_to_all | solution.py:176
  325.5 152.2 %copy-start.73 = (bf16[1024,16]{0,1:T(8,128)(2,1)}, bf16[1024,16]{0,1:T(8,128)(2,1)S(1)}, u32[]{:S(2)}) copy-start(bf16[1024,16]{0,1:T(8,128)(2,1)S(1)} %reshape.567) | copy-start | bytes 98308
  388.5 19.4 %all-to-all-start.1 = ((bf16[4,144,1024]{2,0,1:T(4,128)(2,1)}), bf16[4,144,1024]{2,0,1:T(4,128)(2,1)S(1)}, u32[]{:S(2)}, u32[]{:S(2)}) async-start(bf16[4,144,1024]{2,0,1:T(4,128)(2,1)} %copy.187), calls=%async_computation.1 | async-start | bytes 2359296 | tf_op jit(solution)/shard_map/all_to_all | solution.py:184
  418.7 20.8 %all-to-all-start.4 = ((bf16[16,36,1024]{2,1,0:T(8,128)(2,1)}), bf16[16,36,1024]{2,1,0:T(8,128)(2,1)}, u32[]{:S(2)}, u32[]{:S(2)}) async-start(bf16[16,36,1024]{2,1,0:T(8,128)(2,1)} %reshape.509), calls=%async_computation.4 | async-start | bytes 2621440 | tf_op jit(solution)/shard_map/all_to_all | solution.py:215
  452.1 19.0 %all-to-all-start.5 = ((bf16[4,144,1024]{2,0,1:T(4,128)(2,1)}), bf16[4,144,1024]{2,0,1:T(4,128)(2,1)}, u32[]{:S(2)}, u32[]{:S(2)}) async-start(bf16[4,144,1024]{2,0,1:T(4,128)(2,1)} %copy.204), calls=%async_computation.5 | async-start | bytes 2359296 | tf_op jit(solution)/shard_map/all_to_all | solution.py:230
  512.2 16.6 %all-to-all-start.3 = ((bf16[4,144,1024]{2,0,1:T(4,128)(2,1)}), bf16[4,144,1024]{2,0,1:T(4,128)(2,1)S(1)}, u32[]{:S(2)}, u32[]{:S(2)}) async-start(bf16[4,144,1024]{2,0,1:T(4,128)(2,1)} %copy.200), calls=%async_computation.3 | async-start | bytes 2359296 | tf_op jit(solution)/shard_map/all_to_all | solution.py:184
  540.9 21.1 %all-to-all-start.6 = ((bf16[16,36,1024]{2,1,0:T(8,128)(2,1)}), bf16[16,36,1024]{2,1,0:T(8,128)(2,1)}, u32[]{:S(2)}, u32[]{:S(2)}) async-start(bf16[16,36,1024]{2,1,0:T(8,128)(2,1)} %reshape.514), calls=%async_computation.6 | async-start | bytes 2621440 | tf_op jit(solution)/shard_map/all_to_all | solution.py:215
  545.4 138.4 %reduce-scatter.25.cloned.1.call-start = ((), (), s32[]{:S(2)}) async-start(), calls=%async_computation.30 | async-start | bytes 540672
  550.0 183.3 %reduce-scatter.23.cloned.1.call-start = ((), (), s32[]{:S(2)}) async-start(), calls=%async_computation.29 | async-start | bytes 4718592 | tf_op jit(solution)/shard_map/reduce_scatter | solution.py:352
  570.7 213.0 %reduce-scatter.21.cloned.1.call-start = ((), (), s32[]{:S(2)}) async-start(), calls=%async_computation.28 | async-start | bytes 4718592 | tf_op jit(solution)/shard_map/reduce_scatter | solution.py:349
  583.7 250.6 %reduce-scatter.19.cloned.1.call-start = ((), (), s32[]{:S(2)}) async-start(), calls=%async_computation.27 | async-start | bytes 4718592 | tf_op jit(solution)/shard_map/reduce_scatter | solution.py:346
  599.3 18.7 %all-to-all-start.7 = ((bf16[4,144,1024]{2,0,1:T(4,128)(2,1)}), bf16[4,144,1024]{2,0,1:T(4,128)(2,1)S(1)}, u32[]{:S(2)}, u32[]{:S(2)}) async-start(bf16[4,144,1024]{2,0,1:T(4,128)(2,1)} %copy.218), calls=%async_computation.7 | async-start | bytes 2359296 | tf_op jit(solution)/shard_map/all_to_all | solution.py:230
  602.9 369.5 %reduce-scatter.15.cloned.1.call-start = ((), (), s32[]{:S(2)}) async-start(), calls=%async_computation.25 | async-start | bytes 2162688 | tf_op jit(solution)/shard_map/reduce_scatter | solution.py:340
  632.1 476.0 %reduce-scatter.13.cloned.1.call-start = ((), (), s32[]{:S(2)}) async-start(), calls=%async_computation.24 | async-start | bytes 2162688 | tf_op jit(solution)/shard_map/reduce_scatter | solution.py:339
  637.6 610.7 %reduce-scatter.11.cloned.1.call-start = ((), (), s32[]{:S(2)}) async-start(), calls=%async_computation.23 | async-start | bytes 4325376 | tf_op jit(solution)/shard_map/reduce_scatter | solution.py:338
  642.0 748.5 %reduce-scatter.17.cloned.1.call-start = ((), (), s32[]{:S(2)}) async-start(), calls=%async_computation.26 | async-start | bytes 4325376 | tf_op jit(solution)/shard_map/reduce_scatter | solution.py:341
  (147 other events, 1918.1 us)
Sparse Core Ops, SparseCore 0:
  11.0 56.7 all-gather.8
  70.9 52.4 all-gather.10
  126.2 55.3 all-gather.12
  184.4 55.2 all-gather.14
  241.1 46.2 all-gather.16
  288.9 46.1 all-gather.18
  336.6 46.0 all-gather.20
  550.1 133.6 reduce-scatter.24
  686.2 47.0 reduce-scatter.22
  735.5 48.1 reduce-scatter.20
  786.1 48.1 reduce-scatter.18
  837.1 135.2 reduce-scatter.14
  975.2 132.7 reduce-scatter.12
  1110.9 137.4 reduce-scatter.10
  1251.1 139.3 reduce-scatter.16
where the time goes:
time: 1410 us; the launch traced here: 1400 us
  waiting for transfers between devices  965 us (68%)
  blocking collectives  179 us (13%)
  matrix products  94 us (7%)
  local copies, waits for them, and re-layouts  84.6 us (6%)
  starting transfers between devices  29.5 us (2%)
  other arithmetic  28.9 us (2%)
  between operations  16.3 us (1%)
    reduce_scatter x1, waiting for transfers between devices, per_device(): lax.psum_scatter(dense_total[4], ('fsdp', 'expert'), scatter_dimension=0,...  142 us
    reduce_scatter x1, waiting for transfers between devices, per_device(): lax.psum_scatter(dense_total[1], ('fsdp', 'expert'), scatter_dimension=0,...  140 us
    reduce_scatter x1, waiting for transfers between devices, per_device(): lax.psum_scatter(dense_total[3], ('fsdp', 'expert'), scatter_dimension=0,...  136 us
    reduce_scatter x1, waiting for transfers between devices, per_device(): lax.psum_scatter(dense_total[2], ('fsdp', 'expert'), scatter_dimension=0,...  136 us
    unnamed x2, blocking collectives  80.7 us
    all_gather x1, blocking collectives, per_device(): lax.all_gather(w_router, ('fsdp', 'expert'), axis=0, tiled=True)  77.6 us
    all_gather x1, waiting for transfers between devices, per_device(): lax.all_gather(w_query, ('fsdp', 'expert'), axis=0, tiled=True)  55.7 us
    all_gather x1, waiting for transfers between devices, per_device(): lax.all_gather(w_key, ('fsdp', 'expert'), axis=0, tiled=True)  53.9 us
  transfers between devices with their start and end apart: 22, of which 20 were waited for; matrix products, arithmetic and copies ran while one was open for 9% of the time, Pallas kernels for 0%

commit v1 on v0

v1 whole, which is shorter than its diff:
```python
import jax
import jax.numpy as jnp
import numpy as np
from jax import lax
from jax.sharding import PartitionSpec as P

HEADS = 16
KV_HEADS = 8
HEAD_DIM = 64
EXPERTS = 16
TOP = 8


EPS = 1e-06


def norm_back(grad, values, inverse, gain):
    unit = values * inverse
    scaled = grad * gain
    back = inverse * (scaled - unit * jnp.mean(scaled * unit, -1, keepdims=True))
    return (back, jnp.sum(grad * unit, 0))


def turn_tables(rows, length):
    half = HEAD_DIM // 2
    places = (np.arange(rows) % length).astype(np.float64)
    rates = 10000.0 ** (-np.arange(half, dtype=np.float64) * 2.0 / HEAD_DIM)
    angle = places[:, None] * rates[None, :]
    return (
        np.cos(angle).astype(np.float32)[:, None, :],
        np.sin(angle).astype(np.float32)[:, None, :],
    )


def rotate(values, cosine, sine):
    half = HEAD_DIM // 2
    first = values[..., :half]
    second = values[..., half:]
    return jnp.concatenate([first * cosine - second * sine, second * cosine + first * sine], -1)


def product(left, right):
    return jnp.dot(left, right, preferred_element_type=jnp.float32)


def inner(left, right):
    return lax.dot_general(
        left, right, (((0,), (0,)), ((), ())), preferred_element_type=jnp.float32
    )


def outer_back(left, right):
    return lax.dot_general(
        left, right, (((1,), (1,)), ((), ())), preferred_element_type=jnp.float32
    )


def per_device(
    tokens,
    segments,
    routes,
    cotangent,
    gain_attn,
    w_query,
    w_key,
    w_value,
    w_out,
    gain_moe,
    w_router,
    expert_gate,
    expert_up,
    expert_down,
):
    micro, length, width = tokens.shape
    rows = micro * length
    hidden_units = expert_gate.shape[2]
    repeat = HEADS // KV_HEADS
    scale = HEAD_DIM ** (-0.5)
    highest = lax.Precision.HIGHEST
    bf16 = jnp.bfloat16
    f32 = jnp.float32
    n_fsdp = lax.axis_size("fsdp")
    n_expert = lax.axis_size("expert")
    local = expert_gate.shape[0]
    own = w_query.shape[0]
    wide_q = HEADS * HEAD_DIM
    wide_k = KV_HEADS * HEAD_DIM
    wide_qkv = wide_q + 2 * wide_k

    n_chip = n_fsdp // 2
    same_core = [[2 * chip + core for chip in range(n_chip)] for core in range(2)]
    other_core = [(index, index ^ 1) for index in range(n_fsdp)]
    first_core = lax.axis_index("fsdp") % 2 == 0

    def across(block, axis, groups=None):
        return lax.all_to_all(
            block, axis, split_axis=0, concat_axis=0, axis_index_groups=groups, tiled=True
        )

    def spread_out(block, axis, groups=None):
        count = lax.axis_size(axis) if groups is None else len(groups[0])
        copies = jnp.broadcast_to(block[None], (count,) + block.shape)
        copies = copies.reshape((count * block.shape[0],) + block.shape[1:])
        return across(copies, axis, groups)

    def columns_of(block):
        return block.transpose(1, 0, 2).reshape(block.shape[1], local * hidden_units)

    experts = lax.all_gather(
        jnp.concatenate(
            [columns_of(expert_gate), columns_of(expert_up), columns_of(expert_down)], 1
        ),
        "fsdp",
        axis=0,
        tiled=True,
    )
    units = local * hidden_units
    pair_weight = experts[:, : 2 * units]
    down_weight = experts[:, 2 * units :]

    packed = jnp.concatenate(
        [
            w_query,
            w_key,
            w_value,
            w_router,
            gain_attn[:, None],
            gain_moe[:, None],
            jnp.zeros((own, 128 - EXPERTS - 2), bf16),
            w_out,
        ],
        1,
    )
    part = spread_out(packed, "fsdp", same_core)

    def whole_of(block):
        mine = spread_out(block, "expert")
        other = lax.ppermute(mine, "fsdp", other_core)
        both = jnp.stack(
            [jnp.where(first_core, mine, other), jnp.where(first_core, other, mine)]
        )
        return (
            both.reshape(2, n_expert, n_chip, own, block.shape[1])
            .transpose(2, 0, 1, 3, 4)
            .reshape(width, block.shape[1])
        )

    front = whole_of(part[:, : wide_qkv + 128])
    out_weight = whole_of(part[:, wide_qkv + 128 :])
    qkv_weight = front[:, :wide_qkv]
    small = front[:, wide_qkv:]
    router_weight = small[:, :EXPERTS]
    gains = small[:, EXPERTS : EXPERTS + 2].astype(f32).T
    first_gain = gains[0]
    second_gain = gains[1]

    source = tokens.reshape(rows, width).astype(f32)
    first_inverse = lax.rsqrt(jnp.mean(source * source, -1, keepdims=True) + EPS)
    first_in = (source * first_inverse * first_gain).astype(bf16)
    segment = segments.reshape(rows)
    places = jnp.arange(rows, dtype=jnp.int32)
    same = (places[:, None] // length) == (places[None, :] // length)
    allowed = (
        same & (places[:, None] >= places[None, :]) & (segment[:, None] == segment[None, :])
    )
    cosine, sine = turn_tables(rows, length)
    qkv = product(first_in, qkv_weight)
    query = rotate(qkv[:, :wide_q].reshape(rows, HEADS, HEAD_DIM), cosine, sine)
    query = query.astype(bf16).reshape(rows, KV_HEADS, repeat, HEAD_DIM)
    key = rotate(
        qkv[:, wide_q : wide_q + wide_k].reshape(rows, KV_HEADS, HEAD_DIM), cosine, sine
    ).astype(bf16)
    value = qkv[:, wide_q + wide_k :].astype(bf16).reshape(rows, KV_HEADS, HEAD_DIM)
    scores = (
        jnp.einsum("sgrd,tgd->grst", query, key, preferred_element_type=f32) * scale
    )
    scores = jnp.where(allowed[None, None], scores, -1e30)
    peak = jnp.max(scores, -1, keepdims=True)
    raised = jnp.exp(scores - peak)
    probs = raised / jnp.sum(raised, -1, keepdims=True)
    probs_kept = probs.astype(bf16)
    context = jnp.einsum("grst,tgd->sgrd", probs_kept, value, preferred_element_type=f32)
    context = context.reshape(rows, wide_q).astype(bf16)
    mixed = source + product(context, out_weight)
    second_inverse = lax.rsqrt(jnp.mean(mixed * mixed, -1, keepdims=True) + EPS)
    second_in = (mixed * second_inverse * second_gain).astype(bf16)

    route = routes.reshape(rows, TOP)
    expert_ids = jnp.arange(EXPERTS, dtype=jnp.int32)
    chosen = jnp.any(route[:, :, None] == expert_ids[None, None, :], 1)
    logits = product(second_in, router_weight)
    top = jnp.max(jnp.where(chosen, logits, -jnp.inf), -1, keepdims=True)
    weight = jnp.where(chosen, jnp.exp(jnp.where(chosen, logits - top, 0.0)), 0.0)
    gates = weight / jnp.sum(weight, -1, keepdims=True)

    def halves(block):
        high = block.astype(bf16)
        return [high, (block - high.astype(f32)).astype(bf16)]

    upstream_kept = cotangent.reshape(rows, width)
    upstream = upstream_kept.astype(f32)
    upstream_all = spread_out(upstream_kept, "expert")
    gates_out = gates.reshape(rows, n_expert, local).transpose(1, 0, 2)
    sent = jnp.concatenate(
        [jnp.broadcast_to(second_in[None], (n_expert, rows, width))]
        + halves(gates_out)
        + [jnp.zeros((n_expert, rows, 128 - 2 * local), bf16)],
        2,
    ).reshape(n_expert * rows, width + 128)
    arrived = lax.all_to_all(sent, "expert", split_axis=0, concat_axis=0, tiled=True)
    tokens_all = arrived[:, :width]
    gates_all = arrived[:, width : width + local].astype(f32) + arrived[
        :, width + local : width + 2 * local
    ].astype(f32)
    count = n_expert * rows
    lane_expert = lax.broadcasted_iota(jnp.int32, (1, units), 1) // hidden_units
    gates_wide = gates_all[:, :1]
    for index in range(1, local):
        gates_wide = jnp.where(lane_expert == index, gates_all[:, index : index + 1], gates_wide)

    pair = product(tokens_all, pair_weight)
    gate = pair[:, :units]
    up = pair[:, units:]
    sigma = jax.nn.sigmoid(gate)
    silu = gate * sigma
    hidden = silu * up
    hidden_gated = (hidden * gates_wide).astype(bf16)
    returned = lax.all_to_all(
        outer_back(hidden_gated, down_weight).astype(bf16),
        "expert",
        split_axis=0,
        concat_axis=0,
        tiled=True,
    )
    down_total = inner(upstream_all, hidden_gated).astype(bf16)
    down_part = lax.psum_scatter(down_total, "fsdp", scatter_dimension=0, tiled=True)
    hidden_raw = product(upstream_all, down_weight)
    meeting = hidden_raw * hidden
    gate_grad_all = jnp.concatenate(
        [
            jnp.sum(
                meeting[:, index * hidden_units : (index + 1) * hidden_units], 1, keepdims=True
            )
            for index in range(local)
        ],
        1,
    )
    hidden_grad = hidden_raw * gates_wide
    gate_back = (hidden_grad * up * sigma * (1.0 + gate * (1.0 - sigma))).astype(bf16)
    up_back = (hidden_grad * silu).astype(bf16)
    pair_back = jnp.concatenate([gate_back, up_back], 1)
    sent_back = jnp.concatenate(
        [outer_back(pair_back, pair_weight).astype(bf16)]
        + halves(gate_grad_all)
        + [jnp.zeros((count, 128 - 2 * local), bf16)],
        1,
    )
    home = lax.all_to_all(sent_back, "expert", split_axis=0, concat_axis=0, tiled=True)
    pair_total = inner(tokens_all, pair_back).astype(bf16)
    home, pair_total = lax.optimization_barrier((home, pair_total))
    pair_part = lax.psum_scatter(pair_total, "fsdp", scatter_dimension=0, tiled=True)

    result = mixed + jnp.sum(returned.reshape(n_expert, rows, width).astype(f32), 0)
    home = home.reshape(n_expert, rows, width + 128).astype(f32)
    gate_grad = home[:, :, width : width + local] + home[:, :, width + local : width + 2 * local]
    gate_grad = gate_grad.transpose(1, 0, 2).reshape(rows, EXPERTS)
    logit_grad = gates * (gate_grad - jnp.sum(gates * gate_grad, -1, keepdims=True))
    router_in_grad = jnp.dot(logit_grad, router_weight.astype(f32).T, precision=highest)
    second_grad = jnp.sum(home[:, :, :width], 0) + router_in_grad
    mixed_back, second_gain_grad = norm_back(second_grad, mixed, second_inverse, second_gain)
    mixed_grad = upstream + mixed_back
    branch_grad = mixed_grad.astype(bf16)
    grad_router = lax.dot_general(
        second_in.astype(f32), logit_grad, (((0,), (0,)), ((), ())), precision=highest
    )

    def to_owners(parts):
        kept = []
        given = []
        for block in parts:
            wide = block.shape[1]
            split = block.astype(bf16).reshape(n_chip, 2, n_expert, own, wide)
            split = split.transpose(1, 2, 0, 3, 4).reshape(2, width // 2, wide)
            kept.append(jnp.where(first_core, split[0], split[1]))
            given.append(jnp.where(first_core, split[1], split[0]))
        kept = jnp.concatenate(kept, 1)
        taken = lax.ppermute(jnp.concatenate(given, 1), "fsdp", other_core)
        pieces = across((kept.astype(f32) + taken.astype(f32)).astype(bf16), "expert")
        pieces = pieces.reshape(n_expert, n_chip * own, -1).astype(f32)
        return jnp.sum(pieces, 0).astype(bf16)

    out_pieces = to_owners(
        [
            inner(context, branch_grad),
            jnp.concatenate(
                [
                    grad_router,
                    second_gain_grad[:, None],
                    jnp.zeros((width, 128 - EXPERTS - 1), f32),
                ],
                1,
            ),
        ]
    )
    context_grad = (
        outer_back(branch_grad, out_weight)
        .astype(bf16)
        .reshape(rows, KV_HEADS, repeat, HEAD_DIM)
    )
    value_grad = jnp.einsum(
        "grst,sgrd->tgd", probs_kept, context_grad, preferred_element_type=f32
    )
    value_grad = value_grad.astype(bf16).reshape(rows, wide_k)
    prob_grad = jnp.einsum("sgrd,tgd->grst", context_grad, value, preferred_element_type=f32)
    score_grad = (
        probs * (prob_grad - jnp.sum(probs * prob_grad, -1, keepdims=True))
    ).astype(bf16)
    query_grad = (
        jnp.einsum("grst,tgd->sgrd", score_grad, key, preferred_element_type=f32) * scale
    )
    key_grad = (
        jnp.einsum("grst,sgrd->tgd", score_grad, query, preferred_element_type=f32) * scale
    )
    query_pre_grad = (
        rotate(query_grad.reshape(rows, HEADS, HEAD_DIM), cosine, -sine)
        .astype(bf16)
        .reshape(rows, wide_q)
    )
    key_pre_grad = rotate(key_grad, cosine, -sine).astype(bf16).reshape(rows, wide_k)
    qkv_grad = jnp.concatenate([query_pre_grad, key_pre_grad, value_grad], 1)
    first_grad = outer_back(qkv_grad, qkv_weight)
    source_back, first_gain_grad = norm_back(first_grad, source, first_inverse, first_gain)
    grad_tokens = mixed_grad + source_back
    qkv_pieces = to_owners(
        [
            inner(first_in, qkv_grad),
            jnp.concatenate([first_gain_grad[:, None], jnp.zeros((width, 127), f32)], 1),
        ]
    )
    dense_pieces = across(jnp.concatenate([qkv_pieces, out_pieces], 1), "fsdp", same_core)
    dense_part = jnp.sum(dense_pieces.reshape(n_chip, own, -1).astype(f32), 0)

    def experts_of(block):
        return (
            block.reshape(block.shape[0], local, hidden_units).transpose(1, 0, 2).astype(f32)
        )

    after = wide_qkv + 128
    return (
        result.astype(bf16).reshape(micro, length, width),
        grad_tokens.reshape(micro, length, width),
        dense_part[:, wide_qkv],
        dense_part[:, :wide_q],
        dense_part[:, wide_q : wide_q + wide_k],
        dense_part[:, wide_q + wide_k : wide_qkv],
        dense_part[:, after : after + width],
        dense_part[:, after + width + EXPERTS],
        dense_part[:, after + width : after + width + EXPERTS],
        experts_of(pair_part[:, :units]),
        experts_of(pair_part[:, units:]),
        experts_of(down_part),
    )


def solution(mesh):
    placed = (
        P(None, ("fsdp", "expert"), None),
        P(None, ("fsdp", "expert"), None),
        P(None, ("fsdp", "expert"), None),
        P(None, ("fsdp", "expert"), None),
        P(("fsdp", "expert")),
        P(("fsdp", "expert"), None),
        P(("fsdp", "expert"), None),
        P(("fsdp", "expert"), None),
        P(("fsdp", "expert"), None),
        P(("fsdp", "expert")),
        P(("fsdp", "expert"), None),
        P("expert", "fsdp", None),
        P("expert", "fsdp", None),
        P("expert", "fsdp", None),
    )
    return jax.shard_map(
        per_device,
        mesh=mesh,
        in_specs=placed,
        out_specs=(
            P(None, ("fsdp", "expert"), None),
            P(None, ("fsdp", "expert"), None),
            P(("fsdp", "expert")),
            P(("fsdp", "expert"), None),
            P(("fsdp", "expert"), None),
            P(("fsdp", "expert"), None),
            P(("fsdp", "expert"), None),
            P(("fsdp", "expert")),
            P(("fsdp", "expert"), None),
            P("expert", "fsdp", None),
            P("expert", "fsdp", None),
            P("expert", "fsdp", None),
        ),
        check_vma=False,
    )
```

time: 1410 us -> 403 us (0.29)
  waiting for transfers between devices: 965 us -> 130 us
  blocking collectives: 179 us -> 50.9 us
  local copies, waits for them, and re-layouts: 84.6 us -> 49.9 us
  matrix products: 94 us -> 75 us
    reduce_scatter x7 -> x1, waiting for transfers between devices: 652 us -> 0.01 us  [per_device(): lax.psum_scatter(pair_total, 'fsdp', scatter_dimension=0, tiled=True)]
    all_gather x7 -> x1, waiting for transfers between devices: 210 us -> 0.02 us  [per_device(): lax.all_gather(jnp.concatenate([columns_of(expert_gate), columns_of(exper...]
    unnamed x2 -> x0, blocking collectives: 80.7 us -> none
    all_gather x1 -> x0, blocking collectives: 77.6 us -> none  [per_device(): lax.all_gather(w_router, ('fsdp', 'expert'), axis=0, tiled=True)]
    all_to_all x7 -> x9, waiting for transfers between devices: 62.9 us -> 126 us  [the longest x6 92.7 us: across(): lax.all_to_all(block, axis, split_axis=0, concat_axis=0, axis_index_group...]
    dot_general x41 -> x11, matrix products: 72.7 us -> 30.8 us  [the longest x5 25.1 us: product(): return jnp.dot(left, right, preferred_element_type=jnp.float32)]
    unnamed x16 -> x4, waiting for transfers between devices: 40.4 us -> 0.05 us
    all_to_all x1, blocking collectives: 20.4 us -> 50.9 us  [across(): lax.all_to_all(block, axis, split_axis=0, concat_axis=0, axis_index_group...]
  transfers between devices with their start and end apart: 22 -> 16, of which waited for: 20 -> 9; matrix products, arithmetic and copies ran while one was open for 9% -> 32% of each run, Pallas kernels for 0% -> 0%
where the time goes in v1:
time: 403 us; the launch traced here: 395 us
  waiting for transfers between devices  130 us (32%)
  matrix products  75 us (19%)
  blocking collectives  50.9 us (13%)
  local copies, waits for them, and re-layouts  49.9 us (12%)
  starting transfers between devices  38 us (9%)
  other arithmetic  35.7 us (9%)
  between operations  15.4 us (4%)
    all_to_all x6, waiting for transfers between devices, across(): lax.all_to_all(block, axis, split_axis=0, concat_axis=0, axis_index_group...  92.7 us
    all_to_all x1, blocking collectives, across(): lax.all_to_all(block, axis, split_axis=0, concat_axis=0, axis_index_group...  50.9 us
    dot_general x5, matrix products, product(): return jnp.dot(left, right, preferred_element_type=jnp.float32)  25.1 us
    all_to_all x6, starting transfers between devices, across(): lax.all_to_all(block, axis, split_axis=0, concat_axis=0, axis_index_group...  24 us
    dot_general x4, matrix products, outer_back(): lax.dot_general(left, right, (((1,), (1,)), ((), ())), preferred_element_...  22.2 us
    dot_general x4, matrix products, inner(): lax.dot_general(left, right, (((0,), (0,)), ((), ())), preferred_element_...  17.9 us
    unnamed x127, local copies, waits for them, and re-layouts  17.4 us
    all_to_all x1, waiting for transfers between devices, per_device(): lax.all_to_all(sent, 'expert', split_axis=0, concat_axis=0, tiled=True)  16 us
  transfers between devices with their start and end apart: 16, of which 9 were waited for; matrix products, arithmetic and copies ran while one was open for 32% of the time, Pallas kernels for 0%

profile of v1, /device:TPU:0, one launch (start us, length us, event | category | flops | bytes accessed | tf_op | source)
XLA Modules:
  0.0 395.3 jit_solution(9347011353556202167)
XLA Ops:
  12.1 50.9 %all_to_all.93 = bf16[4,32,3200]{2,1,0:T(8,128)(2,1)S(1)} all-to-all(bf16[4,32,3200]{2,1,0:T(8,128)(2,1)S(1)} %broadcast_in_dim.162), channel_id=1, replica_groups={{0,8,16,24},{4,12,20,28},{1,9,17,25},{5,13,21,29},{2,10,18,26},{6,14,22..., dimensions={0} | all-to-all | bytes 1638400 | tf_op jit(solution)/shard_map/all_to_all | solution.py:96
  64.6 4.5 %all-to-all-start.1 = ((bf16[4,128,2176]{2,1,0:T(8,128)(2,1)}), bf16[4,128,2176]{2,1,0:T(8,128)(2,1)}, u32[]{:S(2)}, u32[]{:S(2)}) async-start(bf16[4,128,2176]{2,1,0:T(8,128)(2,1)} %broadcast_in_dim.163), calls=%async_computation.1 | async-start | bytes 4456448 | tf_op jit(solution)/shard_map/all_to_all | solution.py:96
  69.2 23.6 %all-to-all-done.1 = bf16[4,128,2176]{2,1,0:T(8,128)(2,1)} async-done(((bf16[4,128,2176]{2,1,0:T(8,128)(2,1)}), bf16[4,128,2176]{2,1,0:T(8,128)(2,1)}, u32[]{:S(2)}, u32[]{:S(2)}) %all-to-all-start.1) | async-done | bytes 2228256 | tf_op jit(solution)/shard_map/all_to_all | solution.py:96
  93.8 3.5 all-to-all-start.2
  97.4 13.0 %all-to-all-done.2 = bf16[4,128,1024]{2,1,0:T(8,128)(2,1)S(1)} async-done(((bf16[4,128,1024]{2,1,0:T(8,128)(2,1)}), bf16[4,128,1024]{2,1,0:T(8,128)(2,1)S(1)}, u32[]{:S(2)}, u32[]{:S(2)}) %all-to-all-start.2) | async-done | bytes 1048608 | tf_op jit(solution)/shard_map/all_to_all | solution.py:96
  113.9 2.7 broadcast_select_fusion.1
  133.3 6.5 %concatenate.76 = bf16[4,128,1152]{1,2,0:T(8,128)(2,1)} concatenate(bf16[4,128,1024]{1,2,0:T(8,128)(2,1)} %broadcast_in_dim.167, bf16[4,128,4]{1,2,0:T(4,128)(2,1)S(1)} %get-tuple-element.117, bf16[4,128,4]{1,2,0:T(4,128)(2,1)S(1)} %get-tuple-element.116, bf16[4,128,120]{1,2,0:T(8,128)(2,1)S(1)} %broadcast_in_dim.170), dimensions={2} | concatenate | bytes 2359296 | tf_op jit(solution)/shard_map/concatenate | solution.py:204
  139.8 4.3 %all-to-all-start.3 = ((bf16[4,128,1152]{1,2,0:T(8,128)(2,1)}), bf16[4,128,1152]{1,2,0:T(8,128)(2,1)}, u32[]{:S(2)}, u32[]{:S(2)}) async-start(bf16[4,128,1152]{1,2,0:T(8,128)(2,1)} %concatenate.76), calls=%async_computation.3 | async-start | bytes 2359296 | tf_op jit(solution)/shard_map/all_to_all | solution.py:210
  144.1 16.0 %all-to-all-done.3 = bf16[4,128,1152]{1,2,0:T(8,128)(2,1)} async-done(((bf16[4,128,1152]{1,2,0:T(8,128)(2,1)}), bf16[4,128,1152]{1,2,0:T(8,128)(2,1)}, u32[]{:S(2)}, u32[]{:S(2)}) %all-to-all-start.3) | async-done | bytes 1179680 | tf_op jit(solution)/shard_map/all_to_all | solution.py:210
  161.2 4.3 %all-to-all-start.5 = ((bf16[4,128,1024]{2,1,0:T(8,128)(2,1)}), bf16[4,128,1024]{2,1,0:T(8,128)(2,1)}, u32[]{:S(2)}, u32[]{:S(2)}) async-start(bf16[4,128,1024]{2,1,0:T(8,128)(2,1)} %broadcast_in_dim.182), calls=%async_computation.5 | async-start | bytes 2097152 | tf_op jit(solution)/shard_map/all_to_all | solution.py:96
  169.8 11.5 %fusion.3 = f32[512,4096]{1,0:T(8,128)} fusion(bf16[1024,6144]{0,1:T(8,128)(2,1)} %all-gather.2.cloned.1.call-done, bf16[512,1152]{1,0:T(8,128)(2,1)} %bitcast.240), kind=kOutput, calls=%fused_computation.4 | convolution fusion | flops 4294967296 | bytes 17825792 | tf_op jit(solution)/shard_map/dot_general | solution.py:43
  181.2 11.2 %multiply_convert_fusion.1 = (bf16[512,2048]{1,0:T(8,128)(2,1)}, bf16[512,2048]{1,0:T(8,128)(2,1)}, f32[512,2048]{1,0:T(8,128)}, bf16[512,2048]{1,0:T(8,128)(2,1)S(1)}) fusion(f32[512,4096]{1,0:T(8,128)} %fusion.3, f32[512]{0:T(512)S(1)} %get-tuple-element.113, f32[512]{0:T(512)S(1)} %get-tuple-element.114, f32[512]{0:T(512)S(1)} %get-tuple-element.115, ...), kind=kOutput, calls=%fused_computation.14 | convolution fusion | flops 2169503744 | bytes 24131584 | tf_op jit(solution)/shard_map/dot_general | solution.py:43
  193.7 5.5 %convert_bitcast_fusion = bf16[1024,2048]{0,1:T(8,128)(2,1)} fusion(bf16[512,2048]{1,0:T(8,128)(2,1)S(1)} %get-tuple-element.121, bf16[512,1024]{1,0:T(8,128)(2,1)} %bitcast.40), kind=kOutput, calls=%fused_computation.12 | convolution fusion | flops 2149580800 | bytes 7340032 | tf_op jit(solution)/shard_map/dot_general | solution.py:47
  199.2 6.7 %copy.306 = bf16[1024,2048]{1,0:T(8,128)(2,1)} copy(bf16[1024,2048]{0,1:T(8,128)(2,1)} %convert_bitcast_fusion) | data formatting | bytes 8388608
  205.9 2.5 slice_reduce_fusion.4
  208.9 10.5 %fusion.14 = bf16[512,1024]{1,0:T(8,128)(2,1)} fusion(bf16[1024,6144]{0,1:T(8,128)(2,1)} %all-gather.2.cloned.1.call-done, bf16[512,2048]{1,0:T(8,128)(2,1)} %get-tuple-element.119, bf16[512,2048]{1,0:T(8,128)(2,1)} %get-tuple-element.118), kind=kOutput, calls=%fused_computation.42 | convolution fusion | flops 4303880192 | bytes 13631488 | tf_op jit(solution)/shard_map/dot_general | solution.py:53
  219.4 3.1 concatenate.80
  222.5 4.3 %all-to-all-start.6 = ((bf16[4,128,1152]{2,1,0:T(8,128)(2,1)}), bf16[4,128,1152]{2,1,0:T(8,128)(2,1)}, u32[]{:S(2)}, u32[]{:S(2)}) async-start(bf16[4,128,1152]{2,1,0:T(8,128)(2,1)} %bitcast.222), calls=%async_computation.6 | async-start | bytes 2359296 | tf_op jit(solution)/shard_map/all_to_all | solution.py:258
  226.8 10.4 %convolution_convert_fusion = bf16[1024,4096]{1,0:T(8,128)(2,1)} fusion(bf16[512,2048]{1,0:T(8,128)(2,1)} %get-tuple-element.119, bf16[512,2048]{1,0:T(8,128)(2,1)} %get-tuple-element.118, bf16[512,1152]{1,0:T(8,128)(2,1)} %bitcast.241), kind=kOutput, calls=%fused_computation.1 | convolution fusion | flops 4307550208 | bytes 13631488 | tf_op jit(solution)/shard_map/dot_general | solution.py:47
  237.2 4.6 %all-to-all-done.6 = bf16[4,128,1152]{2,1,0:T(8,128)(2,1)} async-done(((bf16[4,128,1152]{2,1,0:T(8,128)(2,1)}), bf16[4,128,1152]{2,1,0:T(8,128)(2,1)}, u32[]{:S(2)}, u32[]{:S(2)}) %all-to-all-start.6) | async-done | bytes 1179680 | tf_op jit(solution)/shard_map/all_to_all | solution.py:258
  241.8 6.2 %fusion.18 = bf16[512,1024]{1,0:T(8,128)(2,1)} fusion(bf16[512,2048]{1,0:T(8,128)(2,1)} %copy-done.58, bf16[1024,6144]{0,1:T(8,128)(2,1)} %all-gather.2.cloned.1.call-done), kind=kOutput, calls=%fused_computation.44 | convolution fusion | flops 2148007936 | bytes 7340032 | tf_op jit(solution)/shard_map/dot_general | solution.py:53
  248.1 4.5 %all-to-all-start.4 = ((bf16[4,128,1024]{2,1,0:T(8,128)(2,1)}), bf16[4,128,1024]{2,1,0:T(8,128)(2,1)}, u32[]{:S(2)}, u32[]{:S(2)}) async-start(bf16[4,128,1024]{2,1,0:T(8,128)(2,1)} %bitcast.246), calls=%async_computation.4 | async-start | bytes 2097152 | tf_op jit(solution)/shard_map/all_to_all | solution.py:228
  253.2 12.5 %all-to-all-done.4 = bf16[4,128,1024]{2,1,0:T(8,128)(2,1)} async-done(((bf16[4,128,1024]{2,1,0:T(8,128)(2,1)}), bf16[4,128,1024]{2,1,0:T(8,128)(2,1)}, u32[]{:S(2)}, u32[]{:S(2)}) %all-to-all-start.4) | async-done | bytes 1048608 | tf_op jit(solution)/shard_map/all_to_all | solution.py:228
  287.7 4.7 %multiply_reduce_fusion.2 = (bf16[1024]{0:T(1024)(128)(2,1)S(1)}, f32[128]{0:T(128)S(1)}, f32[128,1024]{1,0:T(8,128)}) fusion(bf16[2,64,1024]{2,1,0:T(8,128)(2,1)S(1)} %copy-done.4, f32[128]{0:T(128)S(1)} %copy-done.53, f32[1024]{0:T(1024)S(1)} %copy-done.39, bf16[1024,2176]{1,0:T(8,128)(2,1)} %bitcast.220, bf16[128,512]{0,1:T(8,128)(2,1)S(1)} %bitcast.272, ...), kind=kOutput, calls=%fused_computation.85 | convolution fusion | flops 539360128 | bytes 5512192 | tf_op jit(solution)/shard_map/dot_general | solution.py:53
  296.6 4.6 %collective-permute-done.3 = bf16[512,1152]{1,0:T(8,128)(2,1)S(1)} collective-permute-done((bf16[512,1152]{1,0:T(8,128)(2,1)S(1)}, bf16[512,1152]{1,0:T(8,128)(2,1)S(1)}, u32[]{:S(2)}, u32[]{:S(2)}) %collective-permute-start.3) | collective-permute-done | bytes 1179680 | tf_op jit(solution)/shard_map/ppermute | solution.py:287
  302.6 4.3 %all-to-all-start.8 = ((bf16[4,128,1152]{2,1,0:T(8,128)(2,1)}), bf16[4,128,1152]{2,1,0:T(8,128)(2,1)}, u32[]{:S(2)}, u32[]{:S(2)}) async-start(bf16[4,128,1152]{2,1,0:T(8,128)(2,1)} %bitcast.221), calls=%async_computation.8 | async-start | bytes 2359296 | tf_op jit(solution)/shard_map/all_to_all | solution.py:96
  306.9 3.6 add_convert_fusion
  310.5 12.0 %all-to-all-done.8 = bf16[4,128,1152]{2,1,0:T(8,128)(2,1)} async-done(((bf16[4,128,1152]{2,1,0:T(8,128)(2,1)}), bf16[4,128,1152]{2,1,0:T(8,128)(2,1)}, u32[]{:S(2)}, u32[]{:S(2)}) %all-to-all-start.8) | async-done | bytes 1179680 | tf_op jit(solution)/shard_map/all_to_all | solution.py:96
  322.5 3.6 all-to-all-start.7
  327.7 24.5 %all-to-all-done.7 = bf16[4,128,2176]{2,1,0:T(8,128)(2,1)S(1)} async-done(((bf16[4,128,2176]{2,1,0:T(8,128)(2,1)}), bf16[4,128,2176]{2,1,0:T(8,128)(2,1)S(1)}, u32[]{:S(2)}, u32[]{:S(2)}) %all-to-all-start.7) | async-done | bytes 2228256 | tf_op jit(solution)/shard_map/all_to_all | solution.py:96
  355.5 3.8 all-to-all-start.9
  360.3 19.7 %all-to-all-done.9 = bf16[4,32,3328]{2,1,0:T(8,128)(2,1)S(1)} async-done(((bf16[4,32,3328]{2,1,0:T(8,128)(2,1)}), bf16[4,32,3328]{2,1,0:T(8,128)(2,1)S(1)}, u32[]{:S(2)}, u32[]{:S(2)}) %all-to-all-start.9) | async-done | bytes 852000 | tf_op jit(solution)/shard_map/all_to_all | solution.py:96
  (258 shorter events, 76.5 us)
Async XLA Ops:
  7.2 162.6 %all-gather.2.cloned.1.call-start = ((), (), s32[]{:S(2)}) async-start(), calls=%async_computation.12 | async-start | bytes 14155776 | tf_op jit(solution)/shard_map/all_gather | solution.py:109
  64.6 28.1 %all-to-all-start.1 = ((bf16[4,128,2176]{2,1,0:T(8,128)(2,1)}), bf16[4,128,2176]{2,1,0:T(8,128)(2,1)}, u32[]{:S(2)}, u32[]{:S(2)}) async-start(bf16[4,128,2176]{2,1,0:T(8,128)(2,1)} %broadcast_in_dim.163), calls=%async_computation.1 | async-start | bytes 4456448 | tf_op jit(solution)/shard_map/all_to_all | solution.py:96
  69.1 41.3 %copy-start.3 = (bf16[2,64,1024]{2,1,0:T(8,128)(2,1)S(1)}, bf16[2,64,1024]{2,1,0:T(8,128)(2,1)}, u32[]{:S(2)}) copy-start(bf16[2,64,1024]{2,1,0:T(8,128)(2,1)} %param.18) | copy-start | bytes 786436
  69.1 42.0 %copy-start.54 = (s32[2,1,64]{2,1,0:T(1,128)S(1)}, s32[2,1,64]{2,1,0:T(1,128)}, u32[]{:S(2)}) copy-start(s32[2,1,64]{2,1,0:T(1,128)} %param.19) | copy-start | bytes 1540
  69.1 42.8 %copy-start.46 = (s32[2,64,8]{1,2,0:T(8,128)S(1)}, s32[2,64,8]{1,2,0:T(8,128)}, u32[]{:S(2)}) copy-start(s32[2,64,8]{1,2,0:T(8,128)} %param.20) | copy-start | bytes 12292
  93.8 16.6 %all-to-all-start.2 = ((bf16[4,128,1024]{2,1,0:T(8,128)(2,1)}), bf16[4,128,1024]{2,1,0:T(8,128)(2,1)S(1)}, u32[]{:S(2)}, u32[]{:S(2)}) async-start(bf16[4,128,1024]{2,1,0:T(8,128)(2,1)} %broadcast_in_dim.166), calls=%async_computation.2 | async-start | bytes 2097152 | tf_op jit(solution)/shard_map/all_to_all | solution.py:96
  97.3 16.5 %collective-permute-start = (bf16[512,2176]{1,0:T(8,128)(2,1)}, bf16[512,2176]{1,0:T(8,128)(2,1)}, u32[]{:S(2)}, u32[]{:S(2)}) collective-permute-start(bf16[512,2176]{1,0:T(8,128)(2,1)} %bitcast.4), channel_id=1, source_target_pairs={{0,4},{4,0},{8,12},{12,8},{16,20},{20,16},{24,28},{28,24},{1,5},{5... | collective-permute-start | bytes 6684680 | tf_op jit(solution)/shard_map/ppermute | solution.py:138
  110.4 2.9 collective-permute-start.1
  110.6 8.4 %copy-start.52 = (f32[128]{0:T(128)}, f32[128]{0:T(128)S(1)}, u32[]{:S(2)}) copy-start(f32[128]{0:T(128)S(1)} %rsqrt.20) | copy-start | bytes 1540
  123.5 4.6 %copy-start.19 = (bf16[128,8,32]{0,2,1:T(8,128)(2,1)}, bf16[128,8,32]{0,2,1:T(8,128)(2,1)S(1)}, u32[]{:S(2)}) copy-start(bf16[128,8,32]{0,2,1:T(8,128)(2,1)S(1)} %get-tuple-element.144) | copy-start | bytes 196612
  123.5 4.6 %copy-start.22 = (bf16[128,8,32]{0,2,1:T(8,128)(2,1)}, bf16[128,8,32]{0,2,1:T(8,128)(2,1)S(1)}, u32[]{:S(2)}) copy-start(bf16[128,8,32]{0,2,1:T(8,128)(2,1)S(1)} %get-tuple-element.145) | copy-start | bytes 196612
  132.2 138.9 %copy-start.26 = (f32[128,16]{0,1:T(8,128)}, f32[128,16]{0,1:T(8,128)S(1)}, u32[]{:S(2)}) copy-start(f32[128,16]{0,1:T(8,128)S(1)} %fusion.47) | copy-start | bytes 24580
  133.3 26.8 %copy-start.8 = (bf16[2,64,1024]{2,1,0:T(8,128)(2,1)S(1)}, bf16[2,64,1024]{2,1,0:T(8,128)(2,1)}, u32[]{:S(2)}) copy-start(bf16[2,64,1024]{2,1,0:T(8,128)(2,1)} %param.21) | copy-start | bytes 786436
  139.8 20.3 %all-to-all-start.3 = ((bf16[4,128,1152]{1,2,0:T(8,128)(2,1)}), bf16[4,128,1152]{1,2,0:T(8,128)(2,1)}, u32[]{:S(2)}, u32[]{:S(2)}) async-start(bf16[4,128,1152]{1,2,0:T(8,128)(2,1)} %concatenate.76), calls=%async_computation.3 | async-start | bytes 2359296 | tf_op jit(solution)/shard_map/all_to_all | solution.py:210
  161.2 20.0 %all-to-all-start.5 = ((bf16[4,128,1024]{2,1,0:T(8,128)(2,1)}), bf16[4,128,1024]{2,1,0:T(8,128)(2,1)}, u32[]{:S(2)}, u32[]{:S(2)}) async-start(bf16[4,128,1024]{2,1,0:T(8,128)(2,1)} %broadcast_in_dim.182), calls=%async_computation.5 | async-start | bytes 2097152 | tf_op jit(solution)/shard_map/all_to_all | solution.py:96
  165.5 217.4 %reduce-scatter.7.cloned.1.call-start = ((), (), s32[]{:S(2)}) async-start(), calls=%async_computation.14 | async-start | bytes 4718592
  222.5 19.3 %all-to-all-start.6 = ((bf16[4,128,1152]{2,1,0:T(8,128)(2,1)}), bf16[4,128,1152]{2,1,0:T(8,128)(2,1)}, u32[]{:S(2)}, u32[]{:S(2)}) async-start(bf16[4,128,1152]{2,1,0:T(8,128)(2,1)} %bitcast.222), calls=%async_computation.6 | async-start | bytes 2359296 | tf_op jit(solution)/shard_map/all_to_all | solution.py:258
  226.8 158.6 %reduce-scatter.5.cloned.1.call-start = ((), (), s32[]{:S(2)}) async-start(), calls=%async_computation.13 | async-start | bytes 9437184 | tf_op jit(solution)/shard_map/reduce_scatter | solution.py:261
  248.1 17.6 %all-to-all-start.4 = ((bf16[4,128,1024]{2,1,0:T(8,128)(2,1)}), bf16[4,128,1024]{2,1,0:T(8,128)(2,1)}, u32[]{:S(2)}, u32[]{:S(2)}) async-start(bf16[4,128,1024]{2,1,0:T(8,128)(2,1)} %bitcast.246), calls=%async_computation.4 | async-start | bytes 2097152 | tf_op jit(solution)/shard_map/all_to_all | solution.py:228
  271.0 4.7 %copy-start.5 = (f32[128,1024]{1,0:T(8,128)S(1)}, f32[128,1024]{1,0:T(8,128)}, u32[]{:S(2)}) copy-start(f32[128,1024]{1,0:T(8,128)} %convert_reduce_fusion) | copy-start | bytes 1572868
  271.0 4.7 %copy-start.9 = (bf16[2,64,1024]{2,1,0:T(8,128)(2,1)S(1)}, bf16[2,64,1024]{2,1,0:T(8,128)(2,1)}, u32[]{:S(2)}) copy-start(bf16[2,64,1024]{2,1,0:T(8,128)(2,1)} %param.21) | copy-start | bytes 786436
  271.0 4.7 %copy-start.34 = (f32[1024]{0:T(1024)S(1)}, f32[1024]{0:T(1024)}, u32[]{:S(2)}) copy-start(f32[1024]{0:T(1024)} %get-tuple-element.108) | copy-start | bytes 12292
  271.0 4.7 %copy-start.50 = (f32[128]{0:T(128)S(1)}, f32[128]{0:T(128)}, u32[]{:S(2)}) copy-start(f32[128]{0:T(128)} %copy-done.49) | copy-start | bytes 1540
  271.7 5.0 %copy-start.47 = (f32[128]{0:T(128)}, f32[128]{0:T(128)S(1)}, u32[]{:S(2)}) copy-start(f32[128]{0:T(128)S(1)} %multiply_reduce_fusion.7) | copy-start | bytes 1540
  287.7 5.0 %copy-start.57 = (bf16[128]{0:T(256)(128)(2,1)S(1)}, bf16[128]{0:T(256)(128)(2,1)}, u32[]{:S(2)}) copy-start(bf16[128]{0:T(256)(128)(2,1)} %pad.10.clone) | copy-start | bytes 772
  287.7 5.2 %copy-start = (bf16[4,2,4,32,2048]{4,3,0,2,1:T(8,128)(2,1)S(1)}, bf16[4,2,4,32,2048]{4,3,0,2,1:T(8,128)(2,1)}, u32[]{:S(2)}) copy-start(bf16[4,2,4,32,2048]{4,3,0,2,1:T(8,128)(2,1)} %copy.315) | copy-start | bytes 12582916
  294.8 12.1 %collective-permute-start.2 = (bf16[512,2176]{1,0:T(8,128)(2,1)}, bf16[512,2176]{1,0:T(8,128)(2,1)}, u32[]{:S(2)}, u32[]{:S(2)}) collective-permute-start(bf16[512,2176]{1,0:T(8,128)(2,1)} %pad_maximum_fusion.3), channel_id=1, source_target_pairs={{0,4},{4,0},{8,12},{12,8},{16,20},{20,16},{24,28},{28,24},{1,5},{5... | collective-permute-start | bytes 6684680 | tf_op jit(solution)/shard_map/ppermute | solution.py:287
  296.1 5.2 %collective-permute-start.3 = (bf16[512,1152]{1,0:T(8,128)(2,1)S(1)}, bf16[512,1152]{1,0:T(8,128)(2,1)S(1)}, u32[]{:S(2)}, u32[]{:S(2)}) collective-permute-start(bf16[512,1152]{1,0:T(8,128)(2,1)S(1)} %pad_maximum_fusion.7), channel_id=1, source_target_pairs={{0,4},{4,0},{8,12},{12,8},{16,20},{20,16},{24,28},{28,24},{1,5},{5... | collective-permute-start | bytes 3538952 | tf_op jit(solution)/shard_map/ppermute | solution.py:287
  302.6 19.9 %all-to-all-start.8 = ((bf16[4,128,1152]{2,1,0:T(8,128)(2,1)}), bf16[4,128,1152]{2,1,0:T(8,128)(2,1)}, u32[]{:S(2)}, u32[]{:S(2)}) async-start(bf16[4,128,1152]{2,1,0:T(8,128)(2,1)} %bitcast.221), calls=%async_computation.8 | async-start | bytes 2359296 | tf_op jit(solution)/shard_map/all_to_all | solution.py:96
  322.5 29.6 %all-to-all-start.7 = ((bf16[4,128,2176]{2,1,0:T(8,128)(2,1)}), bf16[4,128,2176]{2,1,0:T(8,128)(2,1)S(1)}, u32[]{:S(2)}, u32[]{:S(2)}) async-start(bf16[4,128,2176]{2,1,0:T(8,128)(2,1)} %bitcast.79), calls=%async_computation.7 | async-start | bytes 4456448 | tf_op jit(solution)/shard_map/all_to_all | solution.py:96
  353.4 5.9 %copy-start.13 = (f32[128,1024]{1,0:T(8,128)S(1)}, f32[128,1024]{1,0:T(8,128)}, u32[]{:S(2)}) copy-start(f32[128,1024]{1,0:T(8,128)} %get-tuple-element.159) | copy-start | bytes 1572868
  355.5 24.5 %all-to-all-start.9 = ((bf16[4,32,3328]{2,1,0:T(8,128)(2,1)}), bf16[4,32,3328]{2,1,0:T(8,128)(2,1)S(1)}, u32[]{:S(2)}, u32[]{:S(2)}) async-start(bf16[4,32,3328]{2,1,0:T(8,128)(2,1)} %bitcast.90), calls=%async_computation.9 | async-start | bytes 1703936 | tf_op jit(solution)/shard_map/all_to_all | solution.py:96
  (43 other events, 75.9 us)
Sparse Core Ops, SparseCore 0:
  11.7 133.8 all-gather.1
  206.1 50.6 reduce-scatter.6
  259.0 87.7 reduce-scatter.4

commit v2 on v1

--- a/solution.py
+++ b/solution.py
@@ -1,7 +1,11 @@
+import functools
+
 import jax
 import jax.numpy as jnp
 import numpy as np
 from jax import lax
+from jax.experimental import pallas as pl
+from jax.experimental.pallas import tpu as pltpu
 from jax.sharding import PartitionSpec as P
 
 HEADS = 16
@@ -53,6 +57,136 @@
     return lax.dot_general(
         left, right, (((1,), (1,)), ((), ())), preferred_element_type=jnp.float32
     )
+
+
+def one_expert(x, u, x_turned, u_turned, weight, gate_column):
+    unit = weight.shape[1] // 3
+    w_gate = weight[:, :unit]
+    w_up = weight[:, unit : 2 * unit]
+    w_down = weight[:, 2 * unit :]
+    gate = product(x, w_gate)
+    up = product(x, w_up)
+    raw = product(u, w_down)
+    sigma = 1.0 / (1.0 + jnp.exp(-gate))
+    silu = gate * sigma
+    hidden = silu * up
+    gate_grad = jnp.sum(raw * hidden, 1, keepdims=True)
+    gated = (hidden * gate_column).astype(jnp.bfloat16)
+    back = raw * gate_column
+    gate_back = (back * up * (sigma + silu * (1.0 - sigma))).astype(jnp.bfloat16)
+    up_back = (back * silu).astype(jnp.bfloat16)
+    return (
+        outer_back(gated, w_down),
+        outer_back(gate_back, w_gate) + outer_back(up_back, w_up),
+        gate_grad,
+        product(x_turned, gate_back).astype(jnp.bfloat16),
+        product(x_turned, up_back).astype(jnp.bfloat16),
+        product(u_turned, gated).astype(jnp.bfloat16),
+    )
+
+
+def pick_gate(block, expert):
+    lane = lax.broadcasted_iota(jnp.int32, block.shape, 1)
+    mine = (lane == expert) | (lane == expert + EXPERTS)
+    return mine, jnp.sum(jnp.where(mine, block, 0.0), 1, keepdims=True)
+
+
+def both_halves(total):
+    lane = lax.broadcasted_iota(jnp.int32, total.shape, 1)
+    high = total.astype(jnp.bfloat16).astype(jnp.float32)
+    return jnp.where(lane < EXPERTS, high, total - high).astype(jnp.bfloat16)
+
+
+def experts_kernel(
+    local, x, gates, u, weight, returned, back, totals, sum_out, sum_back, sum_gate, x_turned, u_turned
+):
+    step = pl.program_id(0)
+    width = x.shape[1]
+
+    @pl.when(step == 0)
+    def _():
+        x_turned[...] = x[...].T
+        u_turned[...] = u[...].T
+        sum_out[...] = jnp.zeros_like(sum_out)
+        sum_back[...] = jnp.zeros_like(sum_back)
+        sum_gate[...] = jnp.zeros_like(sum_gate)
+
+    expert = lax.axis_index("expert") * local + step
+    mine, gate_column = pick_gate(gates[...].astype(jnp.float32), expert)
+    out, token_back, gate_grad, gate_total, up_total, down_total = one_expert(
+        x[...], u[...], x_turned[...], u_turned[...], weight[...], gate_column
+    )
+    unit = weight.shape[1] // 3
+    totals[:, :unit] = gate_total
+    totals[:, unit : 2 * unit] = up_total
+    totals[:, 2 * unit :] = down_total
+    sum_out[...] += out
+    sum_back[...] += token_back
+    sum_gate[...] += jnp.where(mine, gate_grad, 0.0)
+
+    @pl.when(step == local - 1)
+    def _():
+        returned[...] = sum_out[...].astype(jnp.bfloat16)
+        back[:, :width] = sum_back[...].astype(jnp.bfloat16)
+        back[:, width:] = both_halves(sum_gate[...])
+
+
+def run_experts(arrived, u, weight, local):
+    count, width = u.shape
+    wide = weight.shape[1] // local
+    bf16 = jnp.bfloat16
+    if count <= 512:
+        return pl.pallas_call(
+            functools.partial(experts_kernel, local),
+            grid=(local,),
+            in_specs=[
+                pl.BlockSpec((count, width), lambda step: (0, 0)),
+                pl.BlockSpec((count, 128), lambda step: (0, width // 128)),
+                pl.BlockSpec((count, width), lambda step: (0, 0)),
+                pl.BlockSpec((width, wide), lambda step: (0, step)),
+            ],
+            out_specs=[
+                pl.BlockSpec((count, width), lambda step: (0, 0)),
+                pl.BlockSpec((count, width + 128), lambda step: (0, 0)),
+                pl.BlockSpec((width, wide), lambda step: (0, step)),
+            ],
+            out_shape=[
+                jax.ShapeDtypeStruct((count, width), bf16),
+                jax.ShapeDtypeStruct((count, width + 128), bf16),
+                jax.ShapeDtypeStruct(weight.shape, bf16),
+            ],
+            scratch_shapes=[
+                pltpu.VMEM((count, width), jnp.float32),
+                pltpu.VMEM((count, width), jnp.float32),
+                pltpu.VMEM((count, 128), jnp.float32),
+                pltpu.VMEM((width, count), bf16),
+                pltpu.VMEM((width, count), bf16),
+            ],
+            compiler_params=pltpu.CompilerParams(vmem_limit_bytes=48 * 1024 * 1024),
+            cost_estimate=pl.CostEstimate(
+                flops=6 * count * width * weight.shape[1],
+                bytes_accessed=4 * width * weight.shape[1],
+                transcendentals=count * weight.shape[1] // 3,
+            ),
+        )(arrived, arrived, u, weight)
+    x = arrived[:, :width]
+    gates = arrived[:, width:].astype(jnp.float32)
+    sum_out = 0.0
+    sum_back = 0.0
+    sum_gate = 0.0
+    totals = []
+    for step in range(local):
+        expert = lax.axis_index("expert") * local + step
+        mine, gate_column = pick_gate(gates, expert)
+        out, token_back, gate_grad, *own_totals = one_expert(
+            x, u, x.T, u.T, weight[:, step * wide : (step + 1) * wide], gate_column
+        )
+        sum_out = sum_out + out
+        sum_back = sum_back + token_back
+        sum_gate = sum_gate + jnp.where(mine, gate_grad, 0.0)
+        totals += own_totals
+    back = jnp.concatenate([sum_back.astype(bf16), both_halves(sum_gate)], 1)
+    return sum_out.astype(bf16), back, jnp.concatenate(totals, 1)
 
 
 def per_device(
@@ -103,21 +237,6 @@
         copies = copies.reshape((count * block.shape[0],) + block.shape[1:])
         return across(copies, axis, groups)
 
-    def columns_of(block):
-        return block.transpose(1, 0, 2).reshape(block.shape[1], local * hidden_units)
-
-    experts = lax.all_gather(
-        jnp.concatenate(
-            [columns_of(expert_gate), columns_of(expert_up), columns_of(expert_down)], 1
-        ),
-        "fsdp",
-        axis=0,
-        tiled=True,
-    )
-    units = local * hidden_units
-    pair_weight = experts[:, : 2 * units]
-    down_weight = experts[:, 2 * units :]
-
     packed = jnp.concatenate(
         [
             w_query,
@@ -133,6 +252,18 @@
     )
     part = spread_out(packed, "fsdp", same_core)
 
+    held_gate, held_up, held_down, part = lax.optimization_barrier(
+        (expert_gate, expert_up, expert_down, part)
+    )
+    experts = lax.all_gather(
+        jnp.concatenate([held_gate, held_up, held_down], 2)
+        .transpose(1, 0, 2)
+        .reshape(held_gate.shape[1], 3 * local * hidden_units),
+        "fsdp",
+        axis=0,
+        tiled=True,
+    )
+
     def whole_of(block):
         mine = spread_out(block, "expert")
         other = lax.ppermute(mine, "fsdp", other_core)
@@ -193,83 +324,37 @@
     weight = jnp.where(chosen, jnp.exp(jnp.where(chosen, logits - top, 0.0)), 0.0)
     gates = weight / jnp.sum(weight, -1, keepdims=True)
 
-    def halves(block):
-        high = block.astype(bf16)
-        return [high, (block - high.astype(f32)).astype(bf16)]
-
     upstream_kept = cotangent.reshape(rows, width)
     upstream = upstream_kept.astype(f32)
-    upstream_all = spread_out(upstream_kept, "expert")
-    gates_out = gates.reshape(rows, n_expert, local).transpose(1, 0, 2)
+    held_upstream, _ = lax.optimization_barrier((upstream_kept, part))
+    upstream_all = spread_out(held_upstream, "expert")
+    gates_high = gates.astype(bf16)
     sent = jnp.concatenate(
-        [jnp.broadcast_to(second_in[None], (n_expert, rows, width))]
-        + halves(gates_out)
-        + [jnp.zeros((n_expert, rows, 128 - 2 * local), bf16)],
-        2,
-    ).reshape(n_expert * rows, width + 128)
-    arrived = lax.all_to_all(sent, "expert", split_axis=0, concat_axis=0, tiled=True)
-    tokens_all = arrived[:, :width]
-    gates_all = arrived[:, width : width + local].astype(f32) + arrived[
-        :, width + local : width + 2 * local
-    ].astype(f32)
-    count = n_expert * rows
-    lane_expert = lax.broadcasted_iota(jnp.int32, (1, units), 1) // hidden_units
-    gates_wide = gates_all[:, :1]
-    for index in range(1, local):
-        gates_wide = jnp.where(lane_expert == index, gates_all[:, index : index + 1], gates_wide)
-
-    pair = product(tokens_all, pair_weight)
-    gate = pair[:, :units]
-    up = pair[:, units:]
-    sigma = jax.nn.sigmoid(gate)
-    silu = gate * sigma
-    hidden = silu * up
-    hidden_gated = (hidden * gates_wide).astype(bf16)
-    returned = lax.all_to_all(
-        outer_back(hidden_gated, down_weight).astype(bf16),
-        "expert",
-        split_axis=0,
-        concat_axis=0,
-        tiled=True,
-    )
-    down_total = inner(upstream_all, hidden_gated).astype(bf16)
-    down_part = lax.psum_scatter(down_total, "fsdp", scatter_dimension=0, tiled=True)
-    hidden_raw = product(upstream_all, down_weight)
-    meeting = hidden_raw * hidden
-    gate_grad_all = jnp.concatenate(
         [
-            jnp.sum(
-                meeting[:, index * hidden_units : (index + 1) * hidden_units], 1, keepdims=True
-            )
-            for index in range(local)
+            second_in,
+            gates_high,
+            (gates - gates_high.astype(f32)).astype(bf16),
+            jnp.zeros((rows, 128 - 2 * EXPERTS), bf16),
         ],
         1,
     )
-    hidden_grad = hidden_raw * gates_wide
-    gate_back = (hidden_grad * up * sigma * (1.0 + gate * (1.0 - sigma))).astype(bf16)
-    up_back = (hidden_grad * silu).astype(bf16)
-    pair_back = jnp.concatenate([gate_back, up_back], 1)
-    sent_back = jnp.concatenate(
-        [outer_back(pair_back, pair_weight).astype(bf16)]
-        + halves(gate_grad_all)
-        + [jnp.zeros((count, 128 - 2 * local), bf16)],
-        1,
-    )
-    home = lax.all_to_all(sent_back, "expert", split_axis=0, concat_axis=0, tiled=True)
-    pair_total = inner(tokens_all, pair_back).astype(bf16)
-    home, pair_total = lax.optimization_barrier((home, pair_total))
-    pair_part = lax.psum_scatter(pair_total, "fsdp", scatter_dimension=0, tiled=True)
-
-    result = mixed + jnp.sum(returned.reshape(n_expert, rows, width).astype(f32), 0)
-    home = home.reshape(n_expert, rows, width + 128).astype(f32)
-    gate_grad = home[:, :, width : width + local] + home[:, :, width + local : width + 2 * local]
-    gate_grad = gate_grad.transpose(1, 0, 2).reshape(rows, EXPERTS)
+    sent, upstream_all = lax.optimization_barrier((sent, upstream_all))
+    arrived = spread_out(sent, "expert")
+
+    produced, sent_back, expert_total = run_experts(arrived, upstream_all, experts, local)
+    home = across(sent_back, "expert")
+    expert_part = lax.psum_scatter(expert_total, "fsdp", scatter_dimension=0, tiled=True)
+
+    home = jnp.sum(home.reshape(n_expert, rows, width + 128).astype(f32), 0)
+    gate_grad = home[:, width : width + EXPERTS] + home[:, width + EXPERTS : width + 2 * EXPERTS]
     logit_grad = gates * (gate_grad - jnp.sum(gates * gate_grad, -1, keepdims=True))
     router_in_grad = jnp.dot(logit_grad, router_weight.astype(f32).T, precision=highest)
-    second_grad = jnp.sum(home[:, :, :width], 0) + router_in_grad
+    second_grad = home[:, :width] + router_in_grad
     mixed_back, second_gain_grad = norm_back(second_grad, mixed, second_inverse, second_gain)
     mixed_grad = upstream + mixed_back
     branch_grad = mixed_grad.astype(bf16)
+    branch_grad, produced = lax.optimization_barrier((branch_grad, produced))
+    returned = across(produced, "expert")
     grad_router = lax.dot_general(
         second_in.astype(f32), logit_grad, (((0,), (0,)), ((), ())), precision=highest
     )
@@ -285,11 +370,13 @@
             given.append(jnp.where(first_core, split[1], split[0]))
         kept = jnp.concatenate(kept, 1)
         taken = lax.ppermute(jnp.concatenate(given, 1), "fsdp", other_core)
-        pieces = across((kept.astype(f32) + taken.astype(f32)).astype(bf16), "expert")
-        pieces = pieces.reshape(n_expert, n_chip * own, -1).astype(f32)
-        return jnp.sum(pieces, 0).astype(bf16)
-
-    out_pieces = to_owners(
+        return (kept.astype(f32) + taken.astype(f32)).astype(bf16)
+
+    def expert_hop(block):
+        pieces = across(block, "expert").reshape(n_expert, n_chip * own, -1)
+        return jnp.sum(pieces.astype(f32), 0).astype(bf16)
+
+    out_half = to_owners(
         [
             inner(context, branch_grad),
             jnp.concatenate(
@@ -315,6 +402,8 @@
     score_grad = (
         probs * (prob_grad - jnp.sum(probs * prob_grad, -1, keepdims=True))
     ).astype(bf16)
+    score_grad, returned = lax.optimization_barrier((score_grad, returned))
+    result = mixed + jnp.sum(returned.reshape(n_expert, rows, width).astype(f32), 0)
     query_grad = (
         jnp.einsum("grst,tgd->sgrd", score_grad, key, preferred_element_type=f32) * scale
     )
@@ -328,37 +417,38 @@
     )
     key_pre_grad = rotate(key_grad, cosine, -sine).astype(bf16).reshape(rows, wide_k)
     qkv_grad = jnp.concatenate([query_pre_grad, key_pre_grad, value_grad], 1)
+    out_pieces = expert_hop(out_half)
+    qkv_grad, out_pieces = lax.optimization_barrier((qkv_grad, out_pieces))
     first_grad = outer_back(qkv_grad, qkv_weight)
     source_back, first_gain_grad = norm_back(first_grad, source, first_inverse, first_gain)
     grad_tokens = mixed_grad + source_back
-    qkv_pieces = to_owners(
+    qkv_half = to_owners(
         [
             inner(first_in, qkv_grad),
             jnp.concatenate([first_gain_grad[:, None], jnp.zeros((width, 127), f32)], 1),
         ]
     )
-    dense_pieces = across(jnp.concatenate([qkv_pieces, out_pieces], 1), "fsdp", same_core)
+    dense_half = jnp.concatenate([expert_hop(qkv_half), out_pieces], 1)
+    dense_pieces = across(dense_half, "fsdp", same_core)
     dense_part = jnp.sum(dense_pieces.reshape(n_chip, own, -1).astype(f32), 0)
-
-    def experts_of(block):
-        return (
-            block.reshape(block.shape[0], local, hidden_units).transpose(1, 0, 2).astype(f32)
-        )
-
-    after = wide_qkv + 128
+    qkv_part = dense_part[:, : wide_qkv + 128]
+    out_part = dense_part[:, wide_qkv + 128 :]
+
+    expert_part = expert_part.reshape(expert_part.shape[0], local, 3, hidden_units)
+    expert_part = expert_part.transpose(2, 1, 0, 3).astype(f32)
     return (
         result.astype(bf16).reshape(micro, length, width),
         grad_tokens.reshape(micro, length, width),
-        dense_part[:, wide_qkv],
-        dense_part[:, :wide_q],
-        dense_part[:, wide_q : wide_q + wide_k],
-        dense_part[:, wide_q + wide_k : wide_qkv],
-        dense_part[:, after : after + width],
-        dense_part[:, after + width + EXPERTS],
-        dense_part[:, after + width : after + width + EXPERTS],
-        experts_of(pair_part[:, :units]),
-        experts_of(pair_part[:, units:]),
-        experts_of(down_part),
+        qkv_part[:, wide_qkv],
+        qkv_part[:, :wide_q],
+        qkv_part[:, wide_q : wide_q + wide_k],
+        qkv_part[:, wide_q + wide_k : wide_qkv],
+        out_part[:, :width],
+        out_part[:, width + EXPERTS],
+        out_part[:, width : width + EXPERTS],
+        expert_part[0],
+        expert_part[1],
+        expert_part[2],
     )
 
 

time: 403 us -> 345 us (0.86); the launches traced: 395 us -> 344 us
  matrix products: 75 us -> 21.2 us
  Pallas kernels: 0 us -> 26.7 us
  blocking collectives: 50.9 us -> 76.6 us
  local copies, waits for them, and re-layouts: 49.9 us -> 33.5 us
  waiting for transfers between devices: 130 us -> 116 us
  starting transfers between devices: 38 us -> 27.3 us
  other arithmetic: 35.7 us -> 27.7 us
    all_to_all x3 -> x0, waiting for transfers between devices: 33.1 us -> none  [the longest x1 16 us: per_device(): lax.all_to_all(sent, 'expert', split_axis=0, concat_axis=0, tiled=True)]
    pallas_call x0 -> x1, Pallas kernels: none -> 26.7 us  [run_experts(): pl.pallas_call(functools.partial(experts_kernel, local), grid=(local,), i...]
    all_to_all x1 -> x3, blocking collectives: 50.9 us -> 76.6 us  [across(): lax.all_to_all(block, axis, split_axis=0, concat_axis=0, axis_index_group...]
    dot_general x5 -> x3, matrix products: 25.1 us -> 3.4 us  [product(): return jnp.dot(left, right, preferred_element_type=jnp.float32)]
    dot_general x4 -> x2, matrix products: 22.2 us -> 5.51 us  [outer_back(): lax.dot_general(left, right, (((1,), (1,)), ((), ())), preferred_element_...]
    dot_general x4 -> x2, matrix products: 17.9 us -> 1.97 us  [inner(): lax.dot_general(left, right, (((0,), (0,)), ((), ())), preferred_element_...]
    all_to_all x3 -> x0, starting transfers between devices: 13.1 us -> none  [the longest x1 4.5 us: per_device(): lax.all_to_all(outer_back(hidden_gated, down_weight).astype(bf16), 'exper...]
    all_to_all x6 -> x7, waiting for transfers between devices: 92.7 us -> 103 us  [across(): lax.all_to_all(block, axis, split_axis=0, concat_axis=0, axis_index_group...]
  transfers between devices with their start and end apart: 16 -> 13, of which waited for: 9 -> 8; matrix products, arithmetic and copies ran while one was open for 32% -> 20% of each run, Pallas kernels for 0% -> 0%
where the time goes in v2:
time: 345 us; the launch traced here: 344 us
  waiting for transfers between devices  116 us (34%)
  blocking collectives  76.6 us (22%)
  local copies, waits for them, and re-layouts  33.5 us (10%)
  other arithmetic  27.7 us (8%)
  starting transfers between devices  27.3 us (8%)
  Pallas kernels  26.7 us (8%)
  matrix products  21.2 us (6%)
  between operations  15.1 us (4%)
    all_to_all x7, waiting for transfers between devices, across(): lax.all_to_all(block, axis, split_axis=0, concat_axis=0, axis_index_group...  103 us
    all_to_all x3, blocking collectives, across(): lax.all_to_all(block, axis, split_axis=0, concat_axis=0, axis_index_group...  76.6 us
    all_to_all x7, starting transfers between devices, across(): lax.all_to_all(block, axis, split_axis=0, concat_axis=0, axis_index_group...  27.1 us
    pallas_call x1, Pallas kernels, run_experts(): pl.pallas_call(functools.partial(experts_kernel, local), grid=(local,), i...  26.7 us
    all_gather x1, waiting for transfers between devices, per_device(): lax.all_gather(jnp.concatenate([held_gate, held_up, held_down], 2).transp...  9.05 us
    unnamed x99, local copies, waits for them, and re-layouts  8.93 us
  transfers between devices with their start and end apart: 13, of which 8 were waited for; matrix products, arithmetic and copies ran while one was open for 20% of the time, Pallas kernels for 0%

profile of v2, /device:TPU:0, one launch (start us, length us, event | category | flops | bytes accessed | tf_op | source)
XLA Modules:
  0.0 344.0 jit_solution(17806016736250303906)
XLA Ops:
  10.7 26.9 %all_to_all.92 = bf16[4,32,3200]{2,1,0:T(8,128)(2,1)S(1)} all-to-all(bf16[4,32,3200]{2,1,0:T(8,128)(2,1)S(1)} %broadcast_in_dim.46), channel_id=1, replica_groups={{0,8,16,24},{4,12,20,28},{1,9,17,25},{5,13,21,29},{2,10,18,26},{6,14,22..., dimensions={0} | all-to-all | bytes 1638400 | tf_op jit(solution)/shard_map/all_to_all | solution.py:230
  40.7 4.5 %all-to-all-start.1 = ((bf16[4,128,2176]{2,1,0:T(8,128)(2,1)}), bf16[4,128,2176]{2,1,0:T(8,128)(2,1)}, u32[]{:S(2)}, u32[]{:S(2)}) async-start(bf16[4,128,2176]{2,1,0:T(8,128)(2,1)} %broadcast_in_dim.47), calls=%async_computation.1 | async-start | bytes 4456448 | tf_op jit(solution)/shard_map/all_to_all | solution.py:230
  45.3 25.7 %all-to-all-done.1 = bf16[4,128,2176]{2,1,0:T(8,128)(2,1)} async-done(((bf16[4,128,2176]{2,1,0:T(8,128)(2,1)}), bf16[4,128,2176]{2,1,0:T(8,128)(2,1)}, u32[]{:S(2)}, u32[]{:S(2)}) %all-to-all-start.1) | async-done | bytes 2228256 | tf_op jit(solution)/shard_map/all_to_all | solution.py:230
  72.1 3.5 %all-to-all-start.2 = ((bf16[4,128,1024]{2,1,0:T(8,128)(2,1)}), bf16[4,128,1024]{2,1,0:T(8,128)(2,1)S(1)}, u32[]{:S(2)}, u32[]{:S(2)}) async-start(bf16[4,128,1024]{2,1,0:T(8,128)(2,1)} %broadcast_in_dim.50), calls=%async_computation.2 | async-start | bytes 2097152 | tf_op jit(solution)/shard_map/all_to_all | solution.py:230
  75.7 13.0 %all-to-all-done.2 = bf16[4,128,1024]{2,1,0:T(8,128)(2,1)S(1)} async-done(((bf16[4,128,1024]{2,1,0:T(8,128)(2,1)}), bf16[4,128,1024]{2,1,0:T(8,128)(2,1)S(1)}, u32[]{:S(2)}, u32[]{:S(2)}) %all-to-all-start.2) | async-done | bytes 1048608 | tf_op jit(solution)/shard_map/all_to_all | solution.py:230
  92.8 3.5 %all-to-all-start.3 = ((bf16[4,128,1024]{2,1,0:T(8,128)(2,1)}), bf16[4,128,1024]{2,1,0:T(8,128)(2,1)S(1)}, u32[]{:S(2)}, u32[]{:S(2)}) async-start(bf16[4,128,1024]{2,1,0:T(8,128)(2,1)} %broadcast_in_dim.98), calls=%async_computation.3 | async-start | bytes 2097152 | tf_op jit(solution)/shard_map/all_to_all | solution.py:230
  98.2 3.5 %broadcast_select_fusion.1 = (bf16[512,2176]{1,0:T(8,128)(2,1)S(1)}, bf16[512,2176]{1,0:T(8,128)(2,1)S(1)}) fusion(bf16[512,2176]{1,0:T(8,128)(2,1)} %collective-permute-done, pred[]{:T(512)S(6)} %eq.56, bf16[4,128,2176]{2,1,0:T(8,128)(2,1)} %all-to-all-done.1), kind=kLoop, calls=%fused_computation.14 | loop fusion | flops 2228224 | bytes 8912897 | tf_op jit(solution)/shard_map/jit(_where)/select_n | solution.py:271
  107.9 2.0 copy.167
  109.9 1.8 copy.166
  113.4 1.8 subtract_convert_fusion.1
  115.1 3.1 fusion.39
  118.2 2.4 convolution_convert_fusion.3
  126.3 19.8 %all_to_all.93 = bf16[4,128,1152]{2,1,0:T(8,128)(2,1)S(1)} all-to-all(bf16[4,128,1152]{2,1,0:T(8,128)(2,1)S(1)} %broadcast_in_dim.99), channel_id=1, replica_groups=mesh['fsdp'=8,'expert'=4] {'expert'}, dimensions={0} | all-to-all | bytes 2359296 | tf_op jit(solution)/shard_map/all_to_all | solution.py:230
  146.1 9.0 %all-gather.2.cloned.1.call-done.weight = bf16[1024,6144]{1,0:T(8,128)(2,1)} async-done(((bf16[128,6144]{1,0:T(8,128)(2,1)}), bf16[1024,6144]{1,0:T(8,128)(2,1)}) %all-gather.2.cloned.1.call-update) | async-done | bytes 12582928 | tf_op jit(solution)/shard_map/all_gather | solution.py:258
  155.1 26.7 %shard_map.265 = (bf16[512,1024]{1,0:T(8,128)(2,1)}, bf16[512,1152]{1,0:T(8,128)(2,1)}, bf16[1024,6144]{1,0:T(8,128)(2,1)}) custom-call(bf16[512,1152]{1,0:T(8,128)(2,1)S(1)} %bitcast.182, bf16[512,1152]{1,0:T(8,128)(2,1)S(1)} %bitcast.183, bf16[512,1024]{1,0:T(8,128)(2,1)S(1)} %bitcast.184, bf16[1024,6144]{1,0:T(8,128)(2,1)} %all-gather.2.cloned.1.call-done.weight), custom_call_target="tpu_custom_call" | custom-call | flops 19327352832 | bytes 25165824 | tf_op jit(solution)/shard_map/pallas_call | solution.py:139
  181.9 3.8 %all-to-all-start.5 = ((bf16[4,128,1152]{2,1,0:T(8,128)(2,1)}), bf16[4,128,1152]{2,1,0:T(8,128)(2,1)S(1)}, u32[]{:S(2)}, u32[]{:S(2)}) async-start(bf16[4,128,1152]{2,1,0:T(8,128)(2,1)} %bitcast.33), calls=%async_computation.5 | async-start | bytes 2359296 | tf_op jit(solution)/shard_map/all_to_all | solution.py:230
  185.8 15.5 %all-to-all-done.5 = bf16[4,128,1152]{2,1,0:T(8,128)(2,1)S(1)} async-done(((bf16[4,128,1152]{2,1,0:T(8,128)(2,1)}), bf16[4,128,1152]{2,1,0:T(8,128)(2,1)S(1)}, u32[]{:S(2)}, u32[]{:S(2)}) %all-to-all-start.5) | async-done | bytes 1179680 | tf_op jit(solution)/shard_map/all_to_all | solution.py:230
  204.7 4.4 %all-to-all-start.6 = ((bf16[4,128,1024]{2,1,0:T(8,128)(2,1)}), bf16[4,128,1024]{2,1,0:T(8,128)(2,1)}, u32[]{:S(2)}, u32[]{:S(2)}) async-start(bf16[4,128,1024]{2,1,0:T(8,128)(2,1)} %bitcast.36), calls=%async_computation.6 | async-start | bytes 2097152 | tf_op jit(solution)/shard_map/all_to_all | solution.py:230
  212.6 2.1 fusion.15
  215.0 1.9 fusion.12
  216.9 5.7 %all-to-all-done.6 = bf16[4,128,1024]{2,1,0:T(8,128)(2,1)} async-done(((bf16[4,128,1024]{2,1,0:T(8,128)(2,1)}), bf16[4,128,1024]{2,1,0:T(8,128)(2,1)}, u32[]{:S(2)}, u32[]{:S(2)}) %all-to-all-start.6) | async-done | bytes 1048608 | tf_op jit(solution)/shard_map/all_to_all | solution.py:230
  223.1 2.6 add_convert_fusion.1
  225.7 3.9 %all-to-all-start.7 = ((bf16[4,128,1152]{2,1,0:T(8,128)(2,1)}), bf16[4,128,1152]{2,1,0:T(8,128)(2,1)S(1)}, u32[]{:S(2)}, u32[]{:S(2)}) async-start(bf16[4,128,1152]{2,1,0:T(8,128)(2,1)} %bitcast.62), calls=%async_computation.7 | async-start | bytes 2359296 | tf_op jit(solution)/shard_map/all_to_all | solution.py:230
  230.0 13.8 %all-to-all-done.7 = bf16[4,128,1152]{2,1,0:T(8,128)(2,1)S(1)} async-done(((bf16[4,128,1152]{2,1,0:T(8,128)(2,1)}), bf16[4,128,1152]{2,1,0:T(8,128)(2,1)S(1)}, u32[]{:S(2)}, u32[]{:S(2)}) %all-to-all-start.7) | async-done | bytes 1179680 | tf_op jit(solution)/shard_map/all_to_all | solution.py:230
  244.8 4.7 %multiply_reduce_fusion.1 = (bf16[1024]{0:T(1024)(128)(2,1)S(1)}, f32[128]{0:T(128)S(1)}, f32[128,1024]{1,0:T(8,128)}) fusion(bf16[2,64,1024]{2,1,0:T(8,128)(2,1)S(1)} %copy-done.7, f32[128]{0:T(128)S(1)} %copy-done.40, f32[1024]{0:T(1024)S(1)} %copy-done.32, bf16[128,2048]{0,1:T(8,128)(2,1)S(1)} %pad_maximum_fusion.3, bf16[1024,2176]{1,0:T(8,128)(2,1)} %bitcast.202), kind=kOutput, calls=%fused_computation.59 | convolution fusion | flops 537787264 | bytes 5512192 | tf_op jit(solution)/shard_map/dot_general | solution.py:57
  252.2 4.3 %collective-permute-done.3 = bf16[512,2176]{1,0:T(8,128)(2,1)S(1)} collective-permute-done((bf16[512,2176]{1,0:T(8,128)(2,1)S(1)}, bf16[512,2176]{1,0:T(8,128)(2,1)S(1)}, u32[]{:S(2)}, u32[]{:S(2)}) %collective-permute-start.3) | collective-permute-done | bytes 2228256 | tf_op jit(solution)/shard_map/ppermute | solution.py:372
  257.1 29.8 %all_to_all.94 = bf16[4,128,2176]{2,1,0:T(8,128)(2,1)S(1)} all-to-all(bf16[4,128,2176]{2,1,0:T(8,128)(2,1)S(1)} %bitcast.192), channel_id=1, replica_groups=mesh['fsdp'=8,'expert'=4] {'expert'}, dimensions={0} | all-to-all | bytes 4456448 | tf_op jit(solution)/shard_map/all_to_all | solution.py:230
  288.3 2.2 pad_maximum_fusion.2
  290.4 3.5 %all-to-all-start.9 = ((bf16[4,32,3328]{2,1,0:T(8,128)(2,1)}), bf16[4,32,3328]{2,1,0:T(8,128)(2,1)S(1)}, u32[]{:S(2)}, u32[]{:S(2)}) async-start(bf16[4,32,3328]{2,1,0:T(8,128)(2,1)} %bitcast.74), calls=%async_computation.9 | async-start | bytes 1703936 | tf_op jit(solution)/shard_map/all_to_all | solution.py:230
  296.7 28.9 %all-to-all-done.9 = bf16[4,32,3328]{2,1,0:T(8,128)(2,1)S(1)} async-done(((bf16[4,32,3328]{2,1,0:T(8,128)(2,1)}), bf16[4,32,3328]{2,1,0:T(8,128)(2,1)S(1)}, u32[]{:S(2)}, u32[]{:S(2)}) %all-to-all-start.9) | async-done | bytes 852000 | tf_op jit(solution)/shard_map/all_to_all | solution.py:230
  330.1 1.8 slice_bitcast_fusion
  331.9 2.7 copy.190
  (207 shorter events, 50.3 us)
Async XLA Ops:
  7.2 30.5 %copy-start.16 = (bf16[4,128,512]{2,1,0:T(8,128)(2,1)S(1)}, bf16[4,128,512]{2,1,0:T(8,128)(2,1)}, u32[]{:S(2)}) copy-start(bf16[4,128,512]{2,1,0:T(8,128)(2,1)} %param.29) | copy-start | bytes 1572868
  7.2 30.4 %copy-start.15 = (bf16[4,128,512]{2,1,0:T(8,128)(2,1)S(1)}, bf16[4,128,512]{2,1,0:T(8,128)(2,1)}, u32[]{:S(2)}) copy-start(bf16[4,128,512]{2,1,0:T(8,128)(2,1)} %param.30) | copy-start | bytes 1572868
  7.2 30.4 %copy-start.14 = (bf16[4,128,512]{2,1,0:T(8,128)(2,1)S(1)}, bf16[4,128,512]{2,1,0:T(8,128)(2,1)}, u32[]{:S(2)}) copy-start(bf16[4,128,512]{2,1,0:T(8,128)(2,1)} %param.31) | copy-start | bytes 1572868
  7.2 147.9 %all-gather.2.cloned.1.call-start = ((), (), s32[]{:S(2)}) async-start(), calls=%async_computation.11 | async-start | bytes 14155776 | tf_op jit(solution)/shard_map/all_gather | solution.py:258
  40.7 30.3 %all-to-all-start.1 = ((bf16[4,128,2176]{2,1,0:T(8,128)(2,1)}), bf16[4,128,2176]{2,1,0:T(8,128)(2,1)}, u32[]{:S(2)}, u32[]{:S(2)}) async-start(bf16[4,128,2176]{2,1,0:T(8,128)(2,1)} %broadcast_in_dim.47), calls=%async_computation.1 | async-start | bytes 4456448 | tf_op jit(solution)/shard_map/all_to_all | solution.py:230
  45.2 43.5 %copy-start.7 = (bf16[2,64,1024]{2,1,0:T(8,128)(2,1)S(1)}, bf16[2,64,1024]{2,1,0:T(8,128)(2,1)}, u32[]{:S(2)}) copy-start(bf16[2,64,1024]{2,1,0:T(8,128)(2,1)} %param.18) | copy-start | bytes 786436
  45.2 44.2 %copy-start.44 = (s32[2,1,64]{2,1,0:T(1,128)S(1)}, s32[2,1,64]{2,1,0:T(1,128)}, u32[]{:S(2)}) copy-start(s32[2,1,64]{2,1,0:T(1,128)} %param.19) | copy-start | bytes 1540
  45.3 44.9 %copy-start.36 = (s32[2,64,8]{1,2,0:T(8,128)S(1)}, s32[2,64,8]{1,2,0:T(8,128)}, u32[]{:S(2)}) copy-start(s32[2,64,8]{1,2,0:T(8,128)} %param.20) | copy-start | bytes 12292
  45.3 46.5 %copy-start.8 = (bf16[2,64,1024]{2,1,0:T(8,128)(2,1)S(1)}, bf16[2,64,1024]{2,1,0:T(8,128)(2,1)}, u32[]{:S(2)}) copy-start(bf16[2,64,1024]{2,1,0:T(8,128)(2,1)} %param.21) | copy-start | bytes 786436
  72.1 16.6 %all-to-all-start.2 = ((bf16[4,128,1024]{2,1,0:T(8,128)(2,1)}), bf16[4,128,1024]{2,1,0:T(8,128)(2,1)S(1)}, u32[]{:S(2)}, u32[]{:S(2)}) async-start(bf16[4,128,1024]{2,1,0:T(8,128)(2,1)} %broadcast_in_dim.50), calls=%async_computation.2 | async-start | bytes 2097152 | tf_op jit(solution)/shard_map/all_to_all | solution.py:230
  75.6 22.6 %collective-permute-start = (bf16[512,2176]{1,0:T(8,128)(2,1)}, bf16[512,2176]{1,0:T(8,128)(2,1)}, u32[]{:S(2)}, u32[]{:S(2)}) collective-permute-start(bf16[512,2176]{1,0:T(8,128)(2,1)} %bitcast.4), channel_id=1, source_target_pairs={{0,4},{4,0},{8,12},{12,8},{16,20},{20,16},{24,28},{28,24},{1,5},{5... | collective-permute-start | bytes 6684680 | tf_op jit(solution)/shard_map/ppermute | solution.py:269
  88.7 7.7 %collective-permute-start.1 = (bf16[512,1024]{1,0:T(8,128)(2,1)S(1)}, bf16[512,1024]{1,0:T(8,128)(2,1)}, u32[]{:S(2)}, u32[]{:S(2)}) collective-permute-start(bf16[512,1024]{1,0:T(8,128)(2,1)S(1)} %bitcast.204), channel_id=1, source_target_pairs={{0,4},{4,0},{8,12},{12,8},{16,20},{20,16},{24,28},{28,24},{1,5},{5... | collective-permute-start | bytes 3145736 | tf_op jit(solution)/shard_map/ppermute | solution.py:269
  88.9 15.1 %copy-start.39 = (f32[128]{0:T(128)}, f32[128]{0:T(128)S(1)}, u32[]{:S(2)}) copy-start(f32[128]{0:T(128)S(1)} %rsqrt.20) | copy-start | bytes 1540
  92.8 33.4 %all-to-all-start.3 = ((bf16[4,128,1024]{2,1,0:T(8,128)(2,1)}), bf16[4,128,1024]{2,1,0:T(8,128)(2,1)S(1)}, u32[]{:S(2)}, u32[]{:S(2)}) async-start(bf16[4,128,1024]{2,1,0:T(8,128)(2,1)} %broadcast_in_dim.98), calls=%async_computation.3 | async-start | bytes 2097152 | tf_op jit(solution)/shard_map/all_to_all | solution.py:230
  96.4 232.0 %reduce-scatter.2.cloned.1.call-start = ((), (), s32[]{:S(2)}) async-start(), calls=%async_computation.12 | async-start | bytes 14155776 | tf_op jit(solution)/shard_map/reduce_scatter | solution.py:346
  98.2 22.4 %copy-start = (bf16[4,2,4,32,1024]{4,3,2,1,0:T(8,128)(2,1)}, bf16[4,2,4,32,1024]{4,3,2,1,0:T(8,128)(2,1)S(1)}, u32[]{:S(2)}) copy-start(bf16[4,2,4,32,1024]{4,3,2,1,0:T(8,128)(2,1)S(1)} %copy.169) | copy-start | bytes 6291460
  122.1 81.3 %copy-start.37 = (f32[128]{0:T(128)}, f32[128]{0:T(128)S(1)}, u32[]{:S(2)}) copy-start(f32[128]{0:T(128)S(1)} %add_rsqrt_fusion.1) | copy-start | bytes 1540
  181.9 19.9 %copy-start.3 = (f32[128,1024]{1,0:T(8,128)S(1)}, f32[128,1024]{1,0:T(8,128)}, u32[]{:S(2)}) copy-start(f32[128,1024]{1,0:T(8,128)} %copy-done.2) | copy-start | bytes 1572868
  181.9 19.9 %copy-start.27 = (f32[1024]{0:T(1024)S(1)}, f32[1024]{0:T(1024)}, u32[]{:S(2)}) copy-start(f32[1024]{0:T(1024)} %get-tuple-element.108) | copy-start | bytes 12292
  181.9 19.4 %all-to-all-start.5 = ((bf16[4,128,1152]{2,1,0:T(8,128)(2,1)}), bf16[4,128,1152]{2,1,0:T(8,128)(2,1)S(1)}, u32[]{:S(2)}, u32[]{:S(2)}) async-start(bf16[4,128,1152]{2,1,0:T(8,128)(2,1)} %bitcast.33), calls=%async_computation.5 | async-start | bytes 2359296 | tf_op jit(solution)/shard_map/all_to_all | solution.py:230
  185.7 17.8 %copy-start.9 = (bf16[2,64,1024]{2,1,0:T(8,128)(2,1)S(1)}, bf16[2,64,1024]{2,1,0:T(8,128)(2,1)}, u32[]{:S(2)}) copy-start(bf16[2,64,1024]{2,1,0:T(8,128)(2,1)} %param.21) | copy-start | bytes 786436
  204.7 17.9 %all-to-all-start.6 = ((bf16[4,128,1024]{2,1,0:T(8,128)(2,1)}), bf16[4,128,1024]{2,1,0:T(8,128)(2,1)}, u32[]{:S(2)}, u32[]{:S(2)}) async-start(bf16[4,128,1024]{2,1,0:T(8,128)(2,1)} %bitcast.36), calls=%async_computation.6 | async-start | bytes 2097152 | tf_op jit(solution)/shard_map/all_to_all | solution.py:230
  212.5 10.5 %collective-permute-start.2 = (bf16[512,1152]{1,0:T(8,128)(2,1)}, bf16[512,1152]{1,0:T(8,128)(2,1)}, u32[]{:S(2)}, u32[]{:S(2)}) collective-permute-start(bf16[512,1152]{1,0:T(8,128)(2,1)} %pad_maximum_fusion.1), channel_id=1, source_target_pairs={{0,4},{4,0},{8,12},{12,8},{16,20},{20,16},{24,28},{28,24},{1,5},{5... | collective-permute-start | bytes 3538952 | tf_op jit(solution)/shard_map/ppermute | solution.py:372
  215.0 7.9 %copy-start.29 = (f32[128,32]{0,1:T(8,128)S(1)}, f32[128,32]{0,1:T(8,128)}, u32[]{:S(2)}) copy-start(f32[128,32]{0,1:T(8,128)} %constant.89) | copy-start | bytes 49156
  225.7 18.1 %all-to-all-start.7 = ((bf16[4,128,1152]{2,1,0:T(8,128)(2,1)}), bf16[4,128,1152]{2,1,0:T(8,128)(2,1)S(1)}, u32[]{:S(2)}, u32[]{:S(2)}) async-start(bf16[4,128,1152]{2,1,0:T(8,128)(2,1)} %bitcast.62), calls=%async_computation.7 | async-start | bytes 2359296 | tf_op jit(solution)/shard_map/all_to_all | solution.py:230
  229.8 14.9 %copy-start.32 = (f32[1024]{0:T(1024)S(1)}, f32[1024]{0:T(1024)}, u32[]{:S(2)}) copy-start(f32[1024]{0:T(1024)} %copy-done.31) | copy-start | bytes 12292
  229.8 14.9 %copy-start.40 = (f32[128]{0:T(128)S(1)}, f32[128]{0:T(128)}, u32[]{:S(2)}) copy-start(f32[128]{0:T(128)} %copy-done.39) | copy-start | bytes 1540
  252.1 4.4 %collective-permute-start.3 = (bf16[512,2176]{1,0:T(8,128)(2,1)S(1)}, bf16[512,2176]{1,0:T(8,128)(2,1)S(1)}, u32[]{:S(2)}, u32[]{:S(2)}) collective-permute-start(bf16[512,2176]{1,0:T(8,128)(2,1)S(1)} %pad_maximum_fusion), channel_id=1, source_target_pairs={{0,4},{4,0},{8,12},{12,8},{16,20},{20,16},{24,28},{28,24},{1,5},{5... | collective-permute-start | bytes 6684680 | tf_op jit(solution)/shard_map/ppermute | solution.py:372
  288.2 7.3 %copy-start.38 = (f32[128]{0:T(128)S(1)}, f32[128]{0:T(128)}, u32[]{:S(2)}) copy-start(f32[128]{0:T(128)} %copy-done.37) | copy-start | bytes 1540
  288.2 7.3 %copy-start.41 = (f32[128]{0:T(128)S(1)}, f32[128]{0:T(128)}, u32[]{:S(2)}) copy-start(f32[128]{0:T(128)} %copy-done.39) | copy-start | bytes 1540
  288.2 7.3 %copy-start.43 = (f32[128]{0:T(128)S(1)}, f32[128]{0:T(128)}, u32[]{:S(2)}) copy-start(f32[128]{0:T(128)} %copy-done.42) | copy-start | bytes 1540
  290.4 35.1 %all-to-all-start.9 = ((bf16[4,32,3328]{2,1,0:T(8,128)(2,1)}), bf16[4,32,3328]{2,1,0:T(8,128)(2,1)S(1)}, u32[]{:S(2)}, u32[]{:S(2)}) async-start(bf16[4,32,3328]{2,1,0:T(8,128)(2,1)} %bitcast.74), calls=%async_computation.9 | async-start | bytes 1703936 | tf_op jit(solution)/shard_map/all_to_all | solution.py:230
  (27 other events, 96.5 us)
Sparse Core Ops, SparseCore 0:
  39.3 115.8 all-gather.1
  182.0 136.9 reduce-scatter.1
